TPU v7x, 128 devices: a whole 4x4x4 slice. The times are simulated.
128 devices in a mesh: gx: 16 (over z, y), gy: 8 (over x, core).
Axes of the slice: x: 4, y: 4, z: 4, core: 2. Of those that a mesh axis runs over, the one named last changes fastest.
Arguments:
- density: float32 [1, 1024, 4096], P(None, 'gy', 'gx'), may hold values from 0.5 to 4
- velocity: float32 [2, 1, 1024, 4096], P(None, None, 'gy', 'gx'), may hold values from -1 to 1
- energy: float32 [1, 1024, 4096], P(None, 'gy', 'gx'), may hold values from 0.5 to 3
- material: int32 [1, 1024, 4096], P(None, 'gy', 'gx'), may hold values from 0 to 2
- limiter: int32 [1, 1024, 4096], P(None, 'gy', 'gx'), may hold values 0 or 1
- owners: int32 [32768], P(('gx', 'gy')), may hold values from 0 to 15, as said below
- dest_tile: int32 [32768], P(('gx', 'gy')), may hold values from 0 to 255, as said below
- tile_shift: float32 [1, 1024], P(None, 'gy'), may hold values from 0.25 to 0.75
Outputs:
- remapped: float32 [4, 1, 1024, 4096], P(None, None, 'gy', 'gx')
Inputs may be any that keep to these rules, and one draw needn't show every extreme that they name: `owners`: within a plane every mesh row of tiles is rotated along x as a whole by a whole number of tiles, at most 1 either way, and the rotation does not fall from one row to the next; so a tile's owner is its own gx index or the one next to it on either side (wrapping). No device sends more than 128 tiles to either neighbour, and in every draw some device sends exactly 128 to its left neighbour and some exactly 128 to its right one. `dest_tile`: numbered like the owner's own tiles; a destination lies in the tile's own plane and row, and every Eulerian tile is the destination of exactly one Lagrangian tile.
All inputs are finite; a program needn't handle non-finite values. No bound on the sum of `limiter` on one device may be relied on, other than what follows from the above.
Results may differ from a plain program's by a relative error of at most 0.0003.
Values sent between devices are 32-bit elements; how exact they have to be, the bound alone decides.
A program may use at most 64 MiB of HBM per device.

v0:
```python
import jax
import jax.numpy as jnp
from jax import lax
from jax.sharding import PartitionSpec as P

TILE = 128


time_step = 0.05


def padded_2(cells, sides, width):
    for axis, dim in sides:
        count = lax.axis_size(axis)
        head = lax.slice_in_dim(cells, 0, width, axis=dim)
        tail = lax.slice_in_dim(cells, cells.shape[dim] - width, cells.shape[dim], axis=dim)
        cells = jnp.concatenate(
            [
                lax.ppermute(tail, axis, [(i, (i + 1) % count) for i in range(count)]),
                cells,
                lax.ppermute(head, axis, [((i + 1) % count, i) for i in range(count)]),
            ],
            axis=dim,
        )
    return cells


def passed_along(value, axis, steps):
    count = lax.axis_size(axis)
    pairs = [(source, (source + steps) % count) for source in range(count)]
    return lax.ppermute(value, axis, pairs)


def heat_ratio(material):
    return jnp.where(material == 0, 1.4, jnp.where(material == 1, 5.0 / 3.0, 3.0)).astype(
        jnp.float32
    )


def corners(grid_field):
    return (
        grid_field[..., :-1, :-1],
        grid_field[..., :-1, 1:],
        grid_field[..., 1:, :-1],
        grid_field[..., 1:, 1:],
    )


def node_velocity(impedance, pressure, speed_x, speed_y):
    weights = corners(impedance)
    pushes = corners(pressure)
    along_x = corners(speed_x)
    along_y = corners(speed_y)
    totals = weights[0] + weights[1] + weights[2] + weights[3]
    moment_x = (
        weights[0] * along_x[0]
        + weights[1] * along_x[1]
        + weights[2] * along_x[2]
        + weights[3] * along_x[3]
    )
    moment_y = (
        weights[0] * along_y[0]
        + weights[1] * along_y[1]
        + weights[2] * along_y[2]
        + weights[3] * along_y[3]
    )
    node_x = (moment_x + (pushes[0] - pushes[1] + pushes[2] - pushes[3])) / totals
    node_y = (moment_y + (pushes[0] + pushes[1] - pushes[2] - pushes[3])) / totals
    return (node_x, node_y)


def cell_update(impedance, pressure, speed_x, speed_y, density, energy_total, node_x, node_y):
    nodes_x = corners(node_x)
    nodes_y = corners(node_y)
    sum_x = nodes_x[0] + nodes_x[1] + nodes_x[2] + nodes_x[3]
    sum_y = nodes_y[0] + nodes_y[1] + nodes_y[2] + nodes_y[3]
    force_x = 0.5 * impedance * (sum_x - 4.0 * speed_x)
    force_y = 0.5 * impedance * (sum_y - 4.0 * speed_y)
    volume_rate = 0.5 * (
        -nodes_x[0]
        - nodes_y[0]
        + nodes_x[1]
        - nodes_y[1]
        - nodes_x[2]
        + nodes_y[2]
        + nodes_x[3]
        + nodes_y[3]
    )
    relaxation = jnp.zeros_like(speed_x)
    for corner in range(4):
        relaxation = (
            relaxation
            + (nodes_x[corner] - speed_x) * nodes_x[corner]
            + (nodes_y[corner] - speed_y) * nodes_y[corner]
        )
    work_rate = -pressure * volume_rate + 0.5 * impedance * relaxation
    conserved = jnp.stack(
        [
            density,
            density * speed_x + time_step * force_x,
            density * speed_y + time_step * force_y,
            energy_total + time_step * work_rate,
        ]
    )
    left_speed = 0.5 * (nodes_x[0] + nodes_x[2])
    right_speed = 0.5 * (nodes_x[1] + nodes_x[3])
    widths = 1.0 + time_step * (right_speed - left_speed)
    return (conserved / widths, left_speed, right_speed)


def minmod(left_side, right_side):
    return jnp.where(
        left_side * right_side > 0,
        jnp.sign(left_side) * jnp.minimum(jnp.abs(left_side), jnp.abs(right_side)),
        0.0,
    )


def centred(left_side, right_side):
    limit_mag = jnp.minimum(
        jnp.minimum(2.0 * jnp.abs(left_side), 2.0 * jnp.abs(right_side)),
        0.5 * jnp.abs(left_side + right_side),
    )
    return jnp.where(left_side * right_side > 0, jnp.sign(left_side) * limit_mag, 0.0)


def limited(values, neighbour_left, neighbour_right, limiter):
    widened = jnp.concatenate([neighbour_left, values, neighbour_right], axis=-1)
    back_diff = values - widened[..., :-2]
    fore_diff = widened[..., 2:] - values
    return jnp.where(limiter == 1, centred(back_diff, fore_diff), minmod(back_diff, fore_diff))


def integrate(values, slopes, left_pos, right_pos):
    cell_pos = jnp.arange(values.shape[-1]).astype(jnp.float32)
    centre = 0.5 * (left_pos + right_pos)
    low_own = jnp.maximum(left_pos, cell_pos)
    high_own = jnp.minimum(right_pos, cell_pos + 1.0)
    span_own = jnp.maximum(high_own - low_own, 0.0)
    offset_own = 0.5 * (high_own + low_own) - centre
    low_next = jnp.maximum(left_pos, cell_pos + 1.0)
    high_next = jnp.minimum(right_pos, cell_pos + 2.0)
    span_next = jnp.maximum(high_next - low_next, 0.0)
    offset_next = 0.5 * (high_next + low_next) - centre
    part_own = span_own[..., None, :] * (values + slopes * offset_own[..., None, :])
    part_next = span_next[..., None, :] * (values + slopes * offset_next[..., None, :])
    empty_col = jnp.zeros_like(part_next[..., :1])
    main_part = part_own + jnp.concatenate([empty_col, part_next[..., :-1]], axis=-1)
    return (main_part, part_next[..., -1])


def wall_rows(padded, width):
    level = lax.axis_index("gy")
    row_total = padded.shape[2]
    row_index = jnp.arange(row_total)
    outside = (row_index < width) & (level == 0) | (row_index >= row_total - width) & (
        level == lax.axis_size("gy") - 1
    )
    return jnp.where(outside[:, None], 0.0, padded)


def on_device(density, velocity, energy, material, limiter, owners, dest_tile, tile_shift):
    planes, rows_dev, cols_dev = density.shape
    segments = cols_dev // TILE
    tile_count = planes * rows_dev * segments
    row_count = planes * rows_dev
    capacity = tile_count // 2
    ratios = heat_ratio(material)
    pressure = (ratios - 1.0) * density * energy
    impedance = density * jnp.sqrt(ratios * (ratios - 1.0) * energy)
    speed_x = velocity[0]
    speed_y = velocity[1]
    energy_total = density * (energy + 0.5 * (speed_x * speed_x + speed_y * speed_y))
    padded = padded_2(jnp.stack([impedance, pressure, speed_x, speed_y]), (("gx", 3), ("gy", 2)), 1)
    padded = wall_rows(padded, 1)
    node_x, node_y = node_velocity(padded[0], padded[1], padded[2], padded[3])
    values, left_speed, right_speed = cell_update(
        impedance, pressure, speed_x, speed_y, density, energy_total, node_x, node_y
    )
    rim_cells = padded_2(values, (("gx", 3),), 1)
    neighbour_left = rim_cells[..., :1]
    neighbour_right = rim_cells[..., -1:]
    slopes = limited(values, neighbour_left, neighbour_right, limiter)
    tile_values = values.reshape(4, tile_count, TILE).transpose(1, 0, 2)
    tile_slopes = slopes.reshape(4, tile_count, TILE).transpose(1, 0, 2)
    cell_pos = jnp.arange(TILE).astype(jnp.float32)
    offsets = jnp.broadcast_to(tile_shift[:, :, None], (planes, rows_dev, segments)).reshape(
        tile_count, 1
    )
    left_pos = cell_pos + offsets + time_step * left_speed.reshape(tile_count, TILE)
    right_pos = cell_pos + 1.0 + offsets + time_step * right_speed.reshape(tile_count, TILE)
    column = lax.axis_index("gx")
    col_count = lax.axis_size("gx")
    step_over = (owners - column) % col_count
    go_right = step_over == 1
    go_left = step_over == col_count - 1
    stays_home = step_over == 0
    rank_left = jnp.cumsum(go_left.astype(jnp.int32)) - 1
    rank_right = jnp.cumsum(go_right.astype(jnp.int32)) - 1
    slot_ids = jnp.where(
        go_left, rank_left, jnp.where(go_right, capacity + rank_right, 2 * capacity)
    )
    label_values = dest_tile.astype(jnp.float32)
    main_part, spill_part = integrate(tile_values, tile_slopes, left_pos, right_pos)
    label_row = jnp.where(cell_pos == 0.0, label_values[:, None], 0.0)
    payload = jnp.concatenate(
        [
            tile_values,
            tile_slopes,
            left_pos[:, None, :],
            right_pos[:, None, :],
            label_row[:, None, :],
        ],
        axis=1,
    )
    send_buffer = (
        jnp.zeros((2 * capacity + 1, 11, TILE), jnp.float32)
        .at[slot_ids]
        .set(payload)[: 2 * capacity]
    )
    widened = padded_2(send_buffer, (("gx", 0),), capacity)
    incoming = jnp.concatenate([widened[:capacity], widened[3 * capacity :]], axis=0)
    incoming_main, incoming_spill = integrate(
        incoming[:, 0:4], incoming[:, 4:8], incoming[:, 8], incoming[:, 9]
    )
    incoming_labels = incoming[:, 10, 0]
    local_targets = jnp.where(stays_home, dest_tile, tile_count)
    all_targets = jnp.concatenate([local_targets, incoming_labels.astype(jnp.int32)])
    all_main = jnp.concatenate([main_part, incoming_main], axis=0)
    all_spill = jnp.concatenate([spill_part, incoming_spill], axis=0)
    gathered = jax.ops.segment_sum(all_main, all_targets, num_segments=tile_count + 1)[:tile_count]
    is_valid = all_targets < tile_count
    at_end = all_targets % segments == segments - 1
    inside_targets = jnp.where(is_valid & jnp.logical_not(at_end), all_targets + 1, tile_count)
    edge_targets = jnp.where(is_valid & at_end, all_targets // segments, row_count)
    inside = jax.ops.segment_sum(all_spill, inside_targets, num_segments=tile_count + 1)[
        :tile_count
    ]
    edge_spill = jax.ops.segment_sum(all_spill, edge_targets, num_segments=row_count + 1)[
        :row_count
    ]
    arrived = passed_along(edge_spill.T, "gx", 1)
    entering = jnp.concatenate(
        [arrived.T[:, None, :], jnp.zeros((row_count, segments - 1, 4), jnp.float32)], axis=1
    ).reshape(tile_count, 4)
    result = gathered.at[:, :, 0].add(inside + entering)
    return result.transpose(1, 0, 2).reshape(4, planes, rows_dev, cols_dev)


def solution(mesh):
    placed = (
        P(None, "gy", "gx"),
        P(None, None, "gy", "gx"),
        P(None, "gy", "gx"),
        P(None, "gy", "gx"),
        P(None, "gy", "gx"),
        P(("gx", "gy")),
        P(("gx", "gy")),
        P(None, "gy"),
    )
    return jax.shard_map(
        on_device, mesh=mesh, in_specs=placed, out_specs=P(None, None, "gy", "gx"), check_vma=False
    )
```

profile of v0, /device:TPU:0, one launch (start us, length us, event | category | flops | bytes accessed | tf_op | source)
XLA Modules:
  0.0 118.4 jit_solution(4212702223565731380)
XLA Ops:
  0.0 1.2 fusion.54
  1.2 1.1 fusion.47
  2.3 1.0 pad_maximum_fusion.3
  3.4 1.7 %collective-permute-start = (f32[4,1,128,1]{3,2,1,0:T(8,128)S(1)}, f32[4,1,128,1]{3,2,1,0:T(8,128)S(1)}, u32[]{:S(2)}, u32[]{:S(2)}) collective-permute-start(f32[4,1,128,1]{3,2,1,0:T(8,128)S(1)} %get-tuple-element.42), channel_id=1, source_target_pairs={{0,8},{8,16},{16,24},{24,32},{32,40},{40,48},{48,56},{56,64},{64,7... | collective-permute-start | bytes 6152 | tf_op jit(solution)/shard_map/ppermute | solution.py:19
  5.2 5.0 %collective-permute-start.1 = (f32[4,1,128,1]{3,2,1,0:T(8,128)S(1)}, f32[4,1,128,1]{3,2,1,0:T(8,128)S(1)}, u32[]{:S(2)}, u32[]{:S(2)}) collective-permute-start(f32[4,1,128,1]{3,2,1,0:T(8,128)S(1)} %get-tuple-element.43), channel_id=1, source_target_pairs={{8,0},{16,8},{24,16},{32,24},{40,32},{48,40},{56,48},{64,56},{72,6... | collective-permute-start | bytes 6152 | tf_op jit(solution)/shard_map/ppermute | solution.py:21
  10.3 0.6 compare_select_fusion.6
  10.8 0.3 reduce-window.16
  11.3 0.3 reduce-window.24
  11.8 0.7 compare_select_fusion.3
  12.5 0.5 broadcast_compare_fusion.4
  13.0 3.4 %collective-permute-done = f32[4,1,128,1]{3,2,1,0:T(8,128)S(1)} collective-permute-done((f32[4,1,128,1]{3,2,1,0:T(8,128)S(1)}, f32[4,1,128,1]{3,2,1,0:T(8,128)S(1)}, u32[]{:S(2)}, u32[]{:S(2)}) %collective-permute-start) | collective-permute-done | bytes 2080 | tf_op jit(solution)/shard_map/ppermute | solution.py:19
  16.5 2.9 %collective-permute-start.3 = (f32[4,1,1,258]{3,2,1,0:T(1,128)S(1)}, f32[4,1,1,258]{3,2,1,0:T(1,128)S(1)}, u32[]{:S(2)}, u32[]{:S(2)}) collective-permute-start(f32[4,1,1,258]{3,2,1,0:T(1,128)S(1)} %get-tuple-element.31), channel_id=1, source_target_pairs={{1,0},{2,1},{3,2},{4,3},{5,4},{6,5},{7,6},{0,7},{9,8},{10,9},{11,1... | collective-permute-start | bytes 12392 | tf_op jit(solution)/shard_map/ppermute | solution.py:21
  19.7 1.0 collective-permute-done.2
  20.8 0.4 maximum_select_fusion
  21.3 0.4 fusion.15
  21.8 0.4 fusion.10
  22.3 0.5 copy-done.2
  22.7 0.2 fusion.35
  22.9 0.4 fusion.43
  23.4 0.8 fusion.56
  24.3 5.4 %collective-permute-start.5 = (f32[4,1,128,1]{3,2,1,0:T(8,128)S(1)}, f32[4,1,128,1]{3,2,1,0:T(8,128)S(1)}, u32[]{:S(2)}, u32[]{:S(2)}) collective-permute-start(f32[4,1,128,1]{3,2,1,0:T(8,128)S(1)} %get-tuple-element.40), channel_id=1, source_target_pairs={{8,0},{16,8},{24,16},{32,24},{40,32},{48,40},{56,48},{64,56},{72,6... | collective-permute-start | bytes 6152 | tf_op jit(solution)/shard_map/ppermute | solution.py:21
  29.6 0.9 subtract_maximum_fusion
  30.6 0.7 mul.404
  31.3 0.7 mul.406
  31.9 4.5 %collective-permute-done.4 = f32[4,1,128,1]{3,2,1,0:T(8,128)S(1)} collective-permute-done((f32[4,1,128,1]{3,2,1,0:T(8,128)}, f32[4,1,128,1]{3,2,1,0:T(8,128)S(1)}, u32[]{:S(2)}, u32[]{:S(2)}) %collective-permute-start.4) | collective-permute-done | bytes 2080 | tf_op jit(solution)/shard_map/ppermute | solution.py:19
  36.4 0.6 select_select_fusion
  37.2 0.8 copy-done.4
  38.1 1.2 fusion.5
  39.6 0.4 copy-done.15
  40.0 2.2 %copy.70 = f32[256,11,128]{2,1,0:T(8,128)} copy(f32[256,11,128]{2,0,1:T(8,128)S(1)} %select_dynamic-update-slice_fusion) | data formatting | bytes 2883584 | tf_op jit(solution)/shard_map/concatenate | solution.py:206
  42.4 0.5 copy-done.16
  42.9 18.9 %scatter_fusion = f32[257,11,128]{2,1,0:T(8,128)S(1)} fusion(f32[257,11,128]{2,1,0:T(8,128)S(1)} %broadcast_in_dim.117, s32[256]{0:T(256)S(1)} %copy-done.16, f32[256,11,128]{2,1,0:T(8,128)} %copy.70), kind=kCustom, calls=%fused_computation | custom fusion | bytes 4326400 | tf_op jit(solution)/shard_map/scatter | solution.py:219
  62.0 0.2 copy.71
  62.3 0.2 copy.72
  62.5 5.4 %collective-permute-start.7 = (f32[128,11,128]{2,0,1:T(8,128)S(1)}, f32[128,11,128]{2,0,1:T(8,128)S(1)}, u32[]{:S(2)}, u32[]{:S(2)}) collective-permute-start(f32[128,11,128]{2,0,1:T(8,128)S(1)} %copy.72), channel_id=1, source_target_pairs={{8,0},{16,8},{24,16},{32,24},{40,32},{48,40},{56,48},{64,56},{72,6... | collective-permute-start | bytes 2162696 | tf_op jit(solution)/shard_map/ppermute | solution.py:21
  67.9 0.4 slice_reduce_fusion.1
  68.3 14.9 %collective-permute-done.6 = f32[128,11,128]{2,0,1:T(8,128)S(1)} collective-permute-done((f32[128,11,128]{2,0,1:T(8,128)S(1)}, f32[128,11,128]{2,0,1:T(8,128)S(1)}, u32[]{:S(2)}, u32[]{:S(2)}) %collective-permute-start.6) | collective-permute-done | bytes 720928 | tf_op jit(solution)/shard_map/ppermute | solution.py:19
  83.7 0.4 slice_reduce_fusion
  84.3 3.6 %scatter_custom_fusion.3 = f32[129,4]{1,0:T(8,128)S(1)} fusion(s32[512]{0:T(512)S(1)} %bitcast.134, f32[512,4]{1,0:T(8,128)S(1)} %copy.74, f32[]{:T(128)} %constant.116.clone.1), kind=kCustom, calls=%fused_computation.127 | custom fusion | flops 2048 | bytes 2068 | tf_op jit(solution)/shard_map/scatter-add | solution.py:239
  87.9 0.6 slice_bitcast_fusion.4
  88.6 0.2 pad_add_fusion
  88.9 3.2 %scatter_custom_fusion.2 = f32[257,4]{1,0:T(8,128)S(1)} fusion(s32[512]{0:T(512)S(1)} %bitcast.133, f32[512,4]{1,0:T(8,128)S(1)} %copy.74, f32[]{:T(128)} %constant.116.clone.1), kind=kCustom, calls=%fused_computation.120 | custom fusion | flops 2048 | bytes 4116 | tf_op jit(solution)/shard_map/scatter-add | solution.py:236
  92.1 0.7 copy.73
  92.9 17.3 %scatter_fusion.1 = f32[257,4,128]{2,1,0:T(4,128)S(1)} fusion(f32[257,4,128]{2,1,0:T(4,128)S(1)} %broadcast_in_dim.115, s32[512]{0:T(512)S(1)} %pad_add_fusion.1, f32[512,4,128]{2,1,0:T(4,128)S(1)} %copy.73), kind=kCustom, calls=%fused_computation.1 | custom fusion | flops 262144 | bytes 3147776 | tf_op jit(solution)/shard_map/scatter-add | solution.py:231
  110.3 0.9 copy.76
  111.4 1.7 %copy.79 = f32[256,4,1]{2,1,0:T(4,128)S(1)} copy(f32[256,4,1]{1,0,2:T(8,128)S(1)} %fusion.33) | data formatting | bytes 8192 | tf_op jit(solution)/shard_map/reshape.30
  113.2 4.3 %scatter-add.29 = f32[256,4,128]{2,1,0:T(4,128)S(1)} dynamic-update-slice(f32[256,4,128]{2,1,0:T(4,128)S(1)} %slice.297, f32[256,4,1]{2,1,0:T(4,128)S(1)} %slice_add_fusion, s32[]{:T(128)} %constant.119.clone.1, s32[]{:T(128)} %constant.119.clone.1, s32[]{:T(128)} %constant.119.clone.1) | dynamic-update-slice | bytes 8196 | tf_op jit(solution)/shard_map/scatter-add | solution.py:246
  117.5 0.9 reshape.1084
  (100 shorter events, 3.3 us)
Async XLA Ops:
  0.0 10.2 %copy-start.8 = (s32[1,128,256]{2,1,0:T(8,128)S(1)}, s32[1,128,256]{2,1,0:T(8,128)}, u32[]{:S(2)}) copy-start(s32[1,128,256]{2,1,0:T(8,128)} %param.14) | copy-start | bytes 393220
  1.2 9.1 %copy-start.19 = (s32[256]{0:T(256)S(1)}, s32[256]{0:T(256)}, u32[]{:S(2)}) copy-start(s32[256]{0:T(256)} %param.16) | copy-start | bytes 3076
  1.2 9.1 %copy-start.20 = (s32[256]{0:T(256)S(1)}, s32[256]{0:T(256)}, u32[]{:S(2)}) copy-start(s32[256]{0:T(256)} %param.15) | copy-start | bytes 3076
  1.2 15.2 %copy-start = (f32[2,1,128,256]{3,2,1,0:T(8,128)S(1)}, f32[2,1,128,256]{3,2,1,0:T(8,128)}, u32[]{:S(2)}) copy-start(f32[2,1,128,256]{3,2,1,0:T(8,128)} %param.11) | copy-start | bytes 786436
  2.3 17.2 %copy-start.1 = (f32[1,128,256]{2,1,0:T(8,128)S(1)}, f32[1,128,256]{2,1,0:T(8,128)}, u32[]{:S(2)}) copy-start(f32[1,128,256]{2,1,0:T(8,128)} %param.10) | copy-start | bytes 393220
  3.3 16.2 %copy-start.21 = (f32[1,128]{1,0:T(1,128)S(1)}, f32[1,128]{1,0:T(1,128)}, u32[]{:S(2)}) copy-start(f32[1,128]{1,0:T(1,128)} %param.17) | copy-start | bytes 1540
  3.4 12.9 %collective-permute-start = (f32[4,1,128,1]{3,2,1,0:T(8,128)S(1)}, f32[4,1,128,1]{3,2,1,0:T(8,128)S(1)}, u32[]{:S(2)}, u32[]{:S(2)}) collective-permute-start(f32[4,1,128,1]{3,2,1,0:T(8,128)S(1)} %get-tuple-element.42), channel_id=1, source_target_pairs={{0,8},{8,16},{16,24},{24,32},{32,40},{40,48},{48,56},{56,64},{64,7... | collective-permute-start | bytes 6152 | tf_op jit(solution)/shard_map/ppermute | solution.py:19
  5.2 11.2 %collective-permute-start.1 = (f32[4,1,128,1]{3,2,1,0:T(8,128)S(1)}, f32[4,1,128,1]{3,2,1,0:T(8,128)S(1)}, u32[]{:S(2)}, u32[]{:S(2)}) collective-permute-start(f32[4,1,128,1]{3,2,1,0:T(8,128)S(1)} %get-tuple-element.43), channel_id=1, source_target_pairs={{8,0},{16,8},{24,16},{32,24},{40,32},{48,40},{56,48},{64,56},{72,6... | collective-permute-start | bytes 6152 | tf_op jit(solution)/shard_map/ppermute | solution.py:21
  10.2 19.5 %copy-start.9 = (f32[128]{0:T(128)}, f32[128]{0:T(128)S(1)}, u32[]{:S(2)}) copy-start(f32[128]{0:T(128)S(1)} %get-tuple-element.59) | copy-start | bytes 1540
  10.2 19.5 %copy-start.17 = (f32[128]{0:T(128)}, f32[128]{0:T(128)S(1)}, u32[]{:S(2)}) copy-start(f32[128]{0:T(128)S(1)} %get-tuple-element.58) | copy-start | bytes 1540
  10.2 19.4 %copy-start.12 = (f32[128]{0:T(128)}, f32[128]{0:T(128)S(1)}, u32[]{:S(2)}) copy-start(f32[128]{0:T(128)S(1)} %iota_convert_fusion) | copy-start | bytes 1540
  16.5 4.3 %collective-permute-start.2 = (f32[4,1,1,258]{3,2,1,0:T(1,128)S(1)}, f32[4,1,1,258]{3,2,1,0:T(1,128)S(1)}, u32[]{:S(2)}, u32[]{:S(2)}) collective-permute-start(f32[4,1,1,258]{3,2,1,0:T(1,128)S(1)} %get-tuple-element.30), channel_id=1, source_target_pairs={{0,1},{1,2},{2,3},{3,4},{4,5},{5,6},{6,7},{7,0},{8,9},{9,10},{10,1... | collective-permute-start | bytes 12392 | tf_op jit(solution)/shard_map/ppermute | solution.py:19
  16.5 4.3 %collective-permute-start.3 = (f32[4,1,1,258]{3,2,1,0:T(1,128)S(1)}, f32[4,1,1,258]{3,2,1,0:T(1,128)S(1)}, u32[]{:S(2)}, u32[]{:S(2)}) collective-permute-start(f32[4,1,1,258]{3,2,1,0:T(1,128)S(1)} %get-tuple-element.31), channel_id=1, source_target_pairs={{1,0},{2,1},{3,2},{4,3},{5,4},{6,5},{7,6},{0,7},{9,8},{10,9},{11,1... | collective-permute-start | bytes 12392 | tf_op jit(solution)/shard_map/ppermute | solution.py:21
  21.8 0.9 copy-start.2
  24.3 12.2 %collective-permute-start.4 = (f32[4,1,128,1]{3,2,1,0:T(8,128)}, f32[4,1,128,1]{3,2,1,0:T(8,128)S(1)}, u32[]{:S(2)}, u32[]{:S(2)}) collective-permute-start(f32[4,1,128,1]{3,2,1,0:T(8,128)} %get-tuple-element.41), channel_id=1, source_target_pairs={{0,8},{8,16},{16,24},{24,32},{32,40},{40,48},{48,56},{56,64},{64,7... | collective-permute-start | bytes 6152 | tf_op jit(solution)/shard_map/ppermute | solution.py:19
  24.3 12.2 %collective-permute-start.5 = (f32[4,1,128,1]{3,2,1,0:T(8,128)S(1)}, f32[4,1,128,1]{3,2,1,0:T(8,128)S(1)}, u32[]{:S(2)}, u32[]{:S(2)}) collective-permute-start(f32[4,1,128,1]{3,2,1,0:T(8,128)S(1)} %get-tuple-element.40), channel_id=1, source_target_pairs={{8,0},{16,8},{24,16},{32,24},{40,32},{48,40},{56,48},{64,56},{72,6... | collective-permute-start | bytes 6152 | tf_op jit(solution)/shard_map/ppermute | solution.py:21
  30.6 6.7 %copy-start.3 = (f32[256,128]{1,0:T(8,128)}, f32[256,128]{1,0:T(8,128)S(1)}, u32[]{:S(2)}) copy-start(f32[256,128]{1,0:T(8,128)S(1)} %div.43) | copy-start | bytes 393220
  37.1 0.9 copy-start.4
  37.1 1.0 copy-start.5
  38.1 1.3 %copy-start.7 = (f32[256,1,128]{2,0,1:T(8,128)S(1)}, f32[256,1,128]{2,0,1:T(8,128)}, u32[]{:S(2)}) copy-start(f32[256,1,128]{2,0,1:T(8,128)} %mul.404) | copy-start | bytes 393220
  38.1 1.3 %copy-start.13 = (f32[128]{0:T(128)S(1)}, f32[128]{0:T(128)}, u32[]{:S(2)}) copy-start(f32[128]{0:T(128)} %copy-done.12) | copy-start | bytes 1540
  38.1 1.4 %copy-start.6 = (f32[256,1,128]{2,0,1:T(8,128)S(1)}, f32[256,1,128]{2,0,1:T(8,128)}, u32[]{:S(2)}) copy-start(f32[256,1,128]{2,0,1:T(8,128)} %mul.406) | copy-start | bytes 393220
  38.1 1.4 %copy-start.10 = (f32[128]{0:T(128)S(1)}, f32[128]{0:T(128)}, u32[]{:S(2)}) copy-start(f32[128]{0:T(128)} %copy-done.9) | copy-start | bytes 1540
  39.2 0.7 copy-start.15
  39.3 0.7 copy-start.22
  42.2 0.7 copy-start.16
  62.2 21.1 %collective-permute-start.6 = (f32[128,11,128]{2,0,1:T(8,128)S(1)}, f32[128,11,128]{2,0,1:T(8,128)S(1)}, u32[]{:S(2)}, u32[]{:S(2)}) collective-permute-start(f32[128,11,128]{2,0,1:T(8,128)S(1)} %copy.71), channel_id=1, source_target_pairs={{0,8},{8,16},{16,24},{24,32},{32,40},{40,48},{48,56},{56,64},{64,7... | collective-permute-start | bytes 2162696 | tf_op jit(solution)/shard_map/ppermute | solution.py:19
  62.5 20.8 %collective-permute-start.7 = (f32[128,11,128]{2,0,1:T(8,128)S(1)}, f32[128,11,128]{2,0,1:T(8,128)S(1)}, u32[]{:S(2)}, u32[]{:S(2)}) collective-permute-start(f32[128,11,128]{2,0,1:T(8,128)S(1)} %copy.72), channel_id=1, source_target_pairs={{8,0},{16,8},{24,16},{32,24},{40,32},{48,40},{56,48},{64,56},{72,6... | collective-permute-start | bytes 2162696 | tf_op jit(solution)/shard_map/ppermute | solution.py:21
  68.3 15.1 %copy-start.11 = (f32[128]{0:T(128)S(1)}, f32[128]{0:T(128)}, u32[]{:S(2)}) copy-start(f32[128]{0:T(128)} %copy-done.9) | copy-start | bytes 1540
  68.3 15.1 %copy-start.14 = (f32[128]{0:T(128)S(1)}, f32[128]{0:T(128)}, u32[]{:S(2)}) copy-start(f32[128]{0:T(128)} %copy-done.12) | copy-start | bytes 1540
  68.3 15.1 %copy-start.18 = (f32[128]{0:T(128)S(1)}, f32[128]{0:T(128)}, u32[]{:S(2)}) copy-start(f32[128]{0:T(128)} %copy-done.17) | copy-start | bytes 1540
  88.6 21.7 %collective-permute-start.8 = (f32[4,128]{0,1:T(8,128)}, f32[4,128]{0,1:T(8,128)}, u32[]{:S(2)}, u32[]{:S(2)}) collective-permute-start(f32[4,128]{0,1:T(8,128)} %slice_bitcast_fusion.4), channel_id=1, source_target_pairs={{0,8},{8,16},{16,24},{24,32},{32,40},{40,48},{48,56},{56,64},{64,7... | collective-permute-start | bytes 6152 | tf_op jit(solution)/shard_map/ppermute | solution.py:31
where the time goes:
time: 119 us; the launch traced here: 118 us
  local copies, waits for them, and re-layouts  37.6 us (32%)
  other arithmetic  35.8 us (30%)
  waiting for transfers between devices  23.9 us (20%)
  starting transfers between devices  20.5 us (17%)
    ppermute x4, waiting for transfers between devices, padded_2(): lax.ppermute(tail, axis, [(i, (i + 1) % count) for i in range(count)])  23.8 us
    scatter x1, local copies, waits for them, and re-layouts, on_device(): send_buffer = jnp.zeros((2 * capacity + 1, 11, TILE), jnp.float32).at[slo...  18.9 us
    ppermute x4, starting transfers between devices, padded_2(): lax.ppermute(head, axis, [((i + 1) % count, i) for i in range(count)])  18.7 us
    scatter-add x1, other arithmetic, on_device(): jax.ops.segment_sum(all_main, all_targets, num_segments=tile_count + 1)  17.3 us
    scatter-add x1, local copies, waits for them, and re-layouts, on_device(): result = gathered.at[:, :, 0].add(inside + entering)  4.26 us
    scatter-add x1, other arithmetic, on_device(): jax.ops.segment_sum(all_spill, edge_targets, num_segments=row_count + 1)  3.62 us
    another operation x3, other arithmetic, on_device(): jnp.stack([impedance, pressure, speed_x, speed_y])  3.24 us
    scatter-add x1, other arithmetic, on_device(): jax.ops.segment_sum(all_spill, inside_targets, num_segments=tile_count + 1)  3.24 us
  transfers between devices with their start and end apart: 9, of which 4 were waited for; matrix products, arithmetic and copies ran while one was open for 23% of the time, Pallas kernels for 0%

commit v1 on v0

v1 whole, which is shorter than its diff:
```python
import functools

import jax
import jax.numpy as jnp
from jax import lax
from jax.experimental import pallas as pl
from jax.experimental.pallas import tpu as pltpu
from jax.sharding import PartitionSpec as P

MESH = pl.DeviceIdType.MESH
TILE = 128
ROWS = 128
COLS = 256
PAD = 8
G = 8
time_step = 0.05

RUNS = ((1, 5), (5, 9), (9, 13), (13, 15))


def by_material(material, first, second, third):
    return jnp.where(material == 0, first, jnp.where(material == 1, second, third))


def cell_state(density, energy, material):
    pressure = by_material(material, 0.4, 2.0 / 3.0, 2.0) * density * energy
    squared = by_material(material, 0.56, 10.0 / 9.0, 6.0) * energy
    return density * jnp.sqrt(squared), pressure


def node_speed(low, high, left):
    weight = low[0] + high[0]
    from_left = low[1] + high[1]
    from_right = low[2] + high[2]
    along_y = low[3] + high[3]
    scale = 1.0 / (left(weight) + weight)
    return (left(from_left) + from_right) * scale, (left(along_y) + along_y) * scale


def remap_parts(density, energy, speed_x, speed_y, impedance, pressure, limiter, nodes, shift, mask, left, right):
    low_x, low_y, high_x, high_y = nodes
    edge_x = low_x + high_x
    edge_y = low_y + high_y
    turn_y = high_y - low_y
    square = low_x * low_x + high_x * high_x + low_y * low_y + high_y * high_y
    next_x = right(edge_x)
    sum_x = edge_x + next_x
    sum_y = edge_y + right(edge_y)
    volume_rate = 0.5 * ((next_x - edge_x) + (turn_y + right(turn_y)))
    relaxation = (square + right(square)) - speed_x * sum_x - speed_y * sum_y
    half = 0.5 * impedance
    work = half * relaxation - pressure * volume_rate
    left_move = (0.5 * time_step) * edge_x
    right_move = (0.5 * time_step) * next_x
    scale = 1.0 / (1.0 + (right_move - left_move))
    total = density * (energy + 0.5 * (speed_x * speed_x + speed_y * speed_y))
    conserved = (
        density,
        density * speed_x + (time_step * half) * (sum_x - 4.0 * speed_x),
        density * speed_y + (time_step * half) * (sum_y - 4.0 * speed_y),
        total + time_step * work,
    )
    reach = jnp.where(limiter == 1, 2.0, 1.0)
    left_pos = shift + left_move
    right_pos = 1.0 + shift + right_move
    centre = 0.5 * (left_pos + right_pos)
    low_own = jnp.maximum(left_pos, 0.0)
    high_own = jnp.minimum(right_pos, 1.0)
    span_own = jnp.where(mask, jnp.maximum(high_own - low_own, 0.0), 0.0)
    offset_own = 0.5 * (high_own + low_own) - centre
    low_next = jnp.maximum(left_pos, 1.0)
    high_next = jnp.minimum(right_pos, 2.0)
    span_next = jnp.where(mask, jnp.maximum(high_next - low_next, 0.0), 0.0)
    offset_next = 0.5 * (high_next + low_next) - centre
    sums = []
    for field in conserved:
        value = field * scale
        back = value - left(value)
        fore = right(back)
        half_sum = 0.5 * (back + fore)
        limit = reach * jnp.minimum(jnp.abs(back), jnp.abs(fore))
        slope = jnp.where(back * fore > 0.0, jnp.maximum(jnp.minimum(half_sum, limit), -limit), 0.0)
        part_own = span_own * (value + slope * offset_own)
        part_next = span_next * (value + slope * offset_next)
        sums.append(part_own + left(part_next))
    return sums


def kernel(
    n_gx, n_gy,
    density_in, velocity_in, energy_in, material_in, limiter_in, owners_ref, dest_ref, shift_ref, out_ref,
    rho, spx, spy, ene, mat, lim, zed, pre, pl_x, pr_x, pl_y, pu_y, node_x, node_y, shift_b, turn_b,
    to_left, to_right, from_left, from_right, base, outer_up, outer_down, from_down, from_up,
    seam_out_l, seam_out_r, seam_in_l, seam_in_r, rim,
    in_sem, out_sem, bulk_send, bulk_recv, row_send, row_recv, seam_send, seam_recv,
):
    gx = lax.axis_index("gx")
    gy = lax.axis_index("gy")
    right_x = lax.rem(gx + 1, n_gx)
    left_x = lax.rem(gx + n_gx - 1, n_gx)
    up_y = lax.rem(gy + 1, n_gy)
    down_y = lax.rem(gy + n_gy - 1, n_gy)

    loads = [
        pltpu.make_async_copy(source, target, in_sem.at[i])
        for i, (source, target) in enumerate(
            (
                (density_in.at[0], rho),
                (energy_in.at[0], ene),
                (material_in.at[0], mat),
                (velocity_in.at[0, 0], spx),
                (velocity_in.at[1, 0], spy),
                (limiter_in.at[0], lim),
            )
        )
    ]
    for load in loads:
        load.start()

    barrier = pltpu.get_barrier_semaphore()
    for target in ((left_x, gy), (right_x, gy), (gx, up_y), (gx, down_y)):
        pl.semaphore_signal(barrier, inc=1, device_id=target, device_id_type=MESH)

    lanes = lax.broadcasted_iota(jnp.int32, (ROWS, TILE), 1)
    rows = lax.broadcasted_iota(jnp.int32, (ROWS, TILE), 0)

    turn_pairs = jnp.where(owners_ref[...] == gx, lax.bitwise_and(dest_ref[...], 1), -1).astype(jnp.float32)
    turn_row = jnp.zeros((8, ROWS), jnp.float32)
    for j in range(2):
        pick = jnp.where(TILE * j + rows == 2 * lanes, 1.0, 0.0)
        turn_row += jnp.dot(
            jnp.broadcast_to(turn_pairs[j : j + 1], (8, TILE)), pick, preferred_element_type=jnp.float32
        )
    turn_row = turn_row[0:1]
    turn_b[...] = jnp.transpose(jnp.broadcast_to(turn_row, (ROWS, ROWS)))
    shift_row = shift_ref[...]
    shift_b[...] = jnp.transpose(jnp.broadcast_to(shift_row, (ROWS, ROWS)))

    def wide(ref, start):
        return jnp.concatenate([ref[0, pl.ds(start, G), :], ref[1, pl.ds(start, G), :]], axis=1)

    def keep(ref, start, value):
        ref[0, pl.ds(start, G), :] = value[:, :TILE]
        ref[1, pl.ds(start, G), :] = value[:, TILE:]

    def left(x):
        return pltpu.roll(x, 1, 1)

    def right(x):
        return pltpu.roll(x, COLS - 1, 1)

    def derive(g, carry=None):
        at = pl.multiple_of(g * G, G)
        density = rho[pl.ds(at, G), :]
        speed_x = spx[pl.ds(at, G), :]
        speed_y = spy[pl.ds(at, G), :]
        impedance, pressure = cell_state(density, ene[pl.ds(at, G), :], mat[pl.ds(at, G), :])
        pad_at = pl.multiple_of(at + PAD, G)
        keep(zed, pad_at, impedance)
        pre[pl.ds(at, G), :] = pressure
        push_x = impedance * speed_x
        push_y = impedance * speed_y
        keep(pl_x, pad_at, push_x + pressure)
        keep(pr_x, pad_at, push_x - pressure)
        keep(pl_y, pad_at, push_y + pressure)
        keep(pu_y, pad_at, push_y - pressure)
        return carry

    def nodes(g, carry=None):
        at = pl.multiple_of(g * G, G)
        low = [wide(ref, at + PAD - 1) for ref in (zed, pl_x, pr_x, pl_y)]
        high = [wide(ref, pl.multiple_of(at + PAD, G)) for ref in (zed, pl_x, pr_x, pu_y)]
        x, y = node_speed(low, high, left)
        keep(node_x, at, x)
        keep(node_y, at, y)
        return carry

    inner = lax.broadcasted_iota(jnp.int32, (G, COLS), 1)
    inner = (inner >= 2) & (inner < COLS - 2)

    def cells(g, carry=None):
        at = pl.multiple_of(g * G, G)
        here = pl.ds(at, G)
        near = [wide(node_x, at), wide(node_y, at), wide(node_x, at + 1), wide(node_y, at + 1)]
        shift = shift_b[here, :]
        sums = remap_parts(
            rho[here, :], ene[here, :], spx[here, :], spy[here, :],
            wide(zed, pl.multiple_of(at + PAD, G)), pre[here, :], lim[here, :], near,
            jnp.concatenate([shift, shift], axis=1), inner, left, right,
        )
        for f in range(4):
            to_left[f, here, :] = sums[f][:, :TILE]
            to_right[f, here, :] = sums[f][:, TILE:]
        return carry

    def over(first, last, step):
        lax.fori_loop(first, last, step, None)

    sends = []

    def send_rows(i, first, count):
        there = pl.ds(first * G, count * G)
        for way, (source, target, device) in enumerate(
            ((to_right, from_left, right_x), (to_left, from_right, left_x))
        ):
            copy = pltpu.make_async_remote_copy(
                src_ref=source.at[:, there, :],
                dst_ref=target.at[:, there, :],
                send_sem=bulk_send.at[way, i],
                recv_sem=bulk_recv.at[way, i],
                device_id=(device, gy),
                device_id_type=MESH,
            )
            copy.start()
            sends.append(copy)

    for load in loads:
        load.wait()

    filler = jnp.ones((G, TILE), jnp.float32)
    for ref in (zed, pl_x, pr_x, pl_y, pu_y):
        for half in range(2):
            ref[half, 0:G, :] = filler
            ref[half, ROWS + PAD : ROWS + PAD + G, :] = filler

    derive(15)
    over(0, 6, derive)
    over(1, 6, nodes)

    for half in range(2):
        for k, ref in enumerate((zed, pl_x, pr_x, pl_y)):
            outer_up[4 * half + k : 4 * half + k + 1, :] = ref[half, ROWS + PAD - 1 : ROWS + PAD, :]
        for k, ref in enumerate((zed, pl_x, pr_x, pu_y)):
            outer_down[4 * half + k : 4 * half + k + 1, :] = ref[half, PAD : PAD + 1, :]

    over(1, 5, cells)

    pl.semaphore_wait(barrier, 4)

    row_copies = []
    for way, (source, target, device) in enumerate(((outer_up, from_down, up_y), (outer_down, from_up, down_y))):
        copy = pltpu.make_async_remote_copy(
            src_ref=source, dst_ref=target, send_sem=row_send.at[way], recv_sem=row_recv.at[way],
            device_id=(gx, device), device_id_type=MESH,
        )
        copy.start()
        row_copies.append(copy)

    send_rows(0, 1, 4)
    for i, (first, last) in enumerate(RUNS[1:3]):
        top = min(last + 1, 15)
        over(first + 1, top, derive)
        over(first + 1, last + 1, nodes)
        over(first, last, cells)
        send_rows(1 + i, first, last - first)
    over(14, 15, derive)
    over(14, 16, nodes)
    over(13, 15, cells)

    packed_l = jnp.zeros((ROWS, TILE), jnp.float32)
    packed_r = jnp.zeros((ROWS, TILE), jnp.float32)
    for f, ref in enumerate((rho, ene, spx, spy, mat, lim)):
        first = ref[:, :TILE].astype(jnp.float32)
        last = ref[:, TILE:].astype(jnp.float32)
        inside = (lanes >= 4 * f) & (lanes < 4 * f + 4)
        packed_l = jnp.where(inside, pltpu.roll(first, 4 * f, 1) if f else first, packed_l)
        packed_r = jnp.where(inside, pltpu.roll(last, 4 * f + 4, 1), packed_r)
    seam_out_l[0:24, :] = jnp.transpose(packed_l)[0:24, :]
    seam_out_r[0:24, :] = jnp.transpose(packed_r)[0:24, :]

    for copy in row_copies:
        copy.wait()
    below = jnp.where(gy == 0, 0.0, from_down[...])
    above = jnp.where(gy == n_gy - 1, 0.0, from_up[...])
    for half in range(2):
        for k, ref in enumerate((zed, pl_x, pr_x, pl_y)):
            ref[half, PAD - 1 : PAD, :] = below[4 * half + k : 4 * half + k + 1, :]
        for k, ref in enumerate((zed, pl_x, pr_x, pu_y)):
            ref[half, ROWS + PAD : ROWS + PAD + 1, :] = above[4 * half + k : 4 * half + k + 1, :]
    outer_turned = jnp.transpose(
        jnp.concatenate([below, above, jnp.zeros((ROWS - 16, TILE), jnp.float32)], axis=0)
    )
    seam_out_l[24:32, :] = outer_turned[0:8, :]
    seam_out_r[24:32, :] = outer_turned[120:128, :]

    seam_copies = []
    for way, (source, target, device) in enumerate(
        ((seam_out_r, seam_in_l, right_x), (seam_out_l, seam_in_r, left_x))
    ):
        copy = pltpu.make_async_remote_copy(
            src_ref=source, dst_ref=target, send_sem=seam_send.at[way], recv_sem=seam_recv.at[way],
            device_id=(device, gy), device_id_type=MESH,
        )
        copy.start()
        seam_copies.append(copy)
    send_rows(3, 13, 2)
    nodes(0)
    nodes(16)
    cells(0)
    cells(15)
    send_rows(4, 0, 1)
    send_rows(5, 15, 1)

    for copy in seam_copies:
        copy.wait()

    sub8 = lax.broadcasted_iota(jnp.int32, (8, TILE), 0)
    lane8 = lax.broadcasted_iota(jnp.int32, (8, TILE), 1)

    def turned(x, by):
        return pltpu.roll(x, by % 8, 0) if by % 8 else x

    def seam_field(f):
        at, off = 8 * (f // 2), 4 * (f % 2)
        slots = []
        for before, after in ((seam_in_l, seam_out_l), (seam_out_r, seam_in_r)):
            head = turned(before[at : at + 8, :], 8 - off)
            tail = turned(after[at : at + 8, :], 4 - off + 8)
            slots.append(jnp.where(sub8 < 4, head, tail))
        return jnp.concatenate(slots, axis=0)

    def seam_outer(column):
        slots = []
        for before, after, b_off in ((seam_in_l, seam_out_l, 4), (seam_out_r, seam_in_r, 4)):
            head = turned(before[24:32, :], b_off)
            tail = turned(after[24:32, :], 4)
            slots.append(jnp.where(sub8 < 4, head, tail)[:, column : column + 1])
        return jnp.concatenate(slots, axis=0)

    density, energy, speed_x, speed_y, material, limiter = [seam_field(f) for f in range(6)]
    impedance, pressure = cell_state(density, energy, material)
    push_x = impedance * speed_x
    push_y = impedance * speed_y
    first_lane = lax.broadcasted_iota(jnp.int32, (16, ROWS), 1)
    at_first = first_lane == 0
    at_last = first_lane == ROWS - 1

    is_before = lax.broadcasted_iota(jnp.int32, (16, 1), 0)
    is_before = lax.rem(is_before, 8) < 4

    def outer_value(k):
        return jnp.where(is_before, seam_outer(4 + k), seam_outer(k))

    mine_l = (impedance, push_x + pressure, push_x - pressure, push_y + pressure)
    mine_u = (impedance, push_x + pressure, push_x - pressure, push_y - pressure)
    under = [jnp.where(at_first, outer_value(k), pltpu.roll(x, 1, 1)) for k, x in enumerate(mine_l)]
    over_it = [jnp.where(at_last, outer_value(8 + k), pltpu.roll(x, ROWS - 1, 1)) for k, x in enumerate(mine_u)]

    def seam_left(x):
        return pltpu.roll(x, 1, 0)

    def seam_right(x):
        return pltpu.roll(x, 15, 0)

    low = node_speed(under, mine_u, seam_left)
    high = node_speed(mine_l, over_it, seam_left)
    sub16 = lax.rem(lax.broadcasted_iota(jnp.int32, (16, ROWS), 0), 8)
    sums = remap_parts(
        density, energy, speed_x, speed_y, impedance, pressure, limiter, low + high,
        jnp.broadcast_to(shift_row, (16, ROWS)), (sub16 >= 2) & (sub16 < 6), seam_left, seam_right,
    )
    stay = turn_row == 0.0
    goes_right = turn_row == 1.0
    goes_left = turn_row == -1.0
    pieces = []
    for f in range(4):
        at_left, at_right = sums[f][0:8], sums[f][8:16]
        moved = jnp.where(goes_right, at_left, jnp.where(goes_left, at_right, 0.0))
        pieces.append(jnp.where(sub8 < 4, moved, jnp.where(stay, at_left, 0.0)))
        pieces.append(jnp.where(sub8 < 4, jnp.where(stay, at_right, 0.0), moved))
    rim[...] = jnp.transpose(jnp.concatenate(pieces + [jnp.zeros((64, ROWS), jnp.float32)], axis=0))

    near_edge = (lane8 < 3) | (lane8 >= TILE - 2)

    def prepare(g, carry):
        here = pl.ds(pl.multiple_of(g * G, G), G)
        turn = turn_b[here, :]
        edge = rim[here, :]
        for f in range(4):
            first, second = to_left[f, here, :], to_right[f, here, :]
            for half in range(2):
                q = 2 * f + half
                if half == 0:
                    value = jnp.where(turn == 0.0, first, jnp.where(turn == 1.0, 0.0, second))
                else:
                    value = jnp.where(turn == 0.0, second, jnp.where(turn == 1.0, first, 0.0))
                extra = pltpu.roll(edge, (2 * TILE - 8 * q - 4) % TILE, 1)
                base[f, here, half * TILE : (half + 1) * TILE] = value + jnp.where(near_edge, extra, 0.0)
        return carry

    def finish(g, carry=None):
        here = pl.ds(pl.multiple_of(g * G, G), G)
        turn = turn_b[here, :]
        for f in range(4):
            base[f, here, :TILE] += jnp.where(turn == 1.0, from_left[f, here, :], 0.0)
            base[f, here, TILE:] += jnp.where(turn == -1.0, from_right[f, here, :], 0.0)
        return carry

    over(0, 16, prepare)

    outs = []
    for i, (first, last) in enumerate(((1, 5), (5, 9), (9, 13), (13, 15), (0, 1), (15, 16))):
        sends[2 * i].wait()
        sends[2 * i + 1].wait()
        over(first, last, finish)
        there = pl.ds(first * G, (last - first) * G)
        out = pltpu.make_async_copy(base.at[:, there, :], out_ref.at[:, 0, there, :], out_sem.at[i])
        out.start()
        outs.append(out)
    for out in outs:
        out.wait()


def on_device(n_gx, n_gy, density, velocity, energy, material, limiter, owners, dest_tile, tile_shift):
    dma = pltpu.SemaphoreType.DMA
    f32 = jnp.float32
    block = pltpu.VMEM((ROWS, COLS), f32)
    padded = pltpu.VMEM((2, ROWS + 2 * PAD, TILE), f32)
    tiles = pltpu.VMEM((4, ROWS, TILE), f32)
    square = pltpu.VMEM((ROWS, TILE), f32)
    small = pltpu.VMEM((8, TILE), f32)
    seam = pltpu.VMEM((32, ROWS), f32)
    any_space = pl.BlockSpec(memory_space=pl.ANY)
    vmem = pl.BlockSpec(memory_space=pltpu.VMEM)
    return pl.pallas_call(
        functools.partial(kernel, n_gx, n_gy),
        out_shape=jax.ShapeDtypeStruct((4, 1, ROWS, COLS), f32),
        in_specs=[any_space] * 5 + [vmem] * 3,
        out_specs=any_space,
        scratch_shapes=[
            block, block, block, block,
            pltpu.VMEM((ROWS, COLS), jnp.int32), pltpu.VMEM((ROWS, COLS), jnp.int32),
            padded, block, padded, padded, padded, padded, padded, padded, square, square,
            tiles, tiles, tiles, tiles, pltpu.VMEM((4, ROWS, COLS), f32),
            small, small, small, small, seam, seam, seam, seam, square,
            dma((6,)), dma((6,)), dma((2, 6)), dma((2, 6)), dma((2,)), dma((2,)), dma((2,)), dma((2,)),
        ],
        compiler_params=pltpu.CompilerParams(
            collective_id=0, has_side_effects=True, vmem_limit_bytes=24 * 1024 * 1024
        ),
    )(
        density, velocity, energy, material, limiter,
        owners.reshape(2, TILE), dest_tile.reshape(2, TILE), tile_shift,
    )


def solution(mesh):
    placed = (
        P(None, "gy", "gx"),
        P(None, None, "gy", "gx"),
        P(None, "gy", "gx"),
        P(None, "gy", "gx"),
        P(None, "gy", "gx"),
        P(("gx", "gy")),
        P(("gx", "gy")),
        P(None, "gy"),
    )
    return jax.shard_map(
        functools.partial(on_device, mesh.shape["gx"], mesh.shape["gy"]),
        mesh=mesh, in_specs=placed, out_specs=P(None, None, "gy", "gx"), check_vma=False,
    )
```

time: 119 us -> 24.8 us (0.21)
  other arithmetic: 35.8 us -> 0 us
  local copies, waits for them, and re-layouts: 37.6 us -> 6.06 us
  waiting for transfers between devices: 23.9 us -> 0 us
  starting transfers between devices: 20.5 us -> 0 us
  Pallas kernels: 0 us -> 18.5 us
    scatter-add x3 -> x0, other arithmetic: 24.2 us -> none  [the longest x1 17.3 us: on_device(): jax.ops.segment_sum(all_main, all_targets, num_segments=tile_count + 1)]
    ppermute x9 -> x0, waiting for transfers between devices: 23.9 us -> none  [the longest x4 23.8 us: padded_2(): lax.ppermute(tail, axis, [(i, (i + 1) % count) for i in range(count)])]
    ppermute x9 -> x0, starting transfers between devices: 20.5 us -> none  [the longest x4 18.7 us: padded_2(): lax.ppermute(head, axis, [((i + 1) % count, i) for i in range(count)])]
    scatter x1 -> x0, local copies, waits for them, and re-layouts: 18.9 us -> none  [on_device(): send_buffer = jnp.zeros((2 * capacity + 1, 11, TILE), jnp.float32).at[slo...]
    pallas_call x0 -> x1, Pallas kernels: none -> 18.5 us  [on_device(): pl.pallas_call(functools.partial(kernel, n_gx, n_gy), out_shape=jax.Shape...]
    scatter-add x1 -> x0, local copies, waits for them, and re-layouts: 4.26 us -> none  [on_device(): result = gathered.at[:, :, 0].add(inside + entering)]
    another operation x9 -> x0, other arithmetic: 3.95 us -> none  [the longest x3 3.24 us: on_device(): jnp.stack([impedance, pressure, speed_x, speed_y])]
    unnamed x49 -> x17, local copies, waits for them, and re-layouts: 2.48 us -> 6.06 us
  transfers between devices with their start and end apart: 9 -> 0, of which waited for: 4 -> 0; matrix products, arithmetic and copies ran while one was open for 23% -> 0% of each run, Pallas kernels for 0% -> 0%
where the time goes in v1:
time: 24.8 us; the launch traced here: 24.6 us
  Pallas kernels  18.5 us (75%)
  local copies, waits for them, and re-layouts  6.06 us (24%)
    pallas_call x1, Pallas kernels, on_device(): pl.pallas_call(functools.partial(kernel, n_gx, n_gy), out_shape=jax.Shape...  18.5 us
    unnamed x17, local copies, waits for them, and re-layouts  6.06 us

profile of v1, /device:TPU:0, one launch (start us, length us, event | category | flops | bytes accessed | tf_op | source)
XLA Modules:
  0.0 24.6 jit_solution(9973765991450710871)
XLA Ops:
  0.0 0.0 copy-start.6
  0.0 0.0 copy-start.5
  0.0 0.0 copy-start.7
  0.0 0.7 %copy-done.6 = s32[256]{0:T(256)S(1)} copy-done((s32[256]{0:T(256)S(1)}, s32[256]{0:T(256)}, u32[]{:S(2)}) %copy-start.6) | copy-done | bytes 1048
  0.7 0.0 copy-done.5
  0.7 0.0 copy-done.7
  0.7 0.0 copy-start
  0.7 0.9 %copy-done = f32[2,1,128,256]{3,2,1,0:T(8,128)S(1)} copy-done((f32[2,1,128,256]{3,2,1,0:T(8,128)S(1)}, f32[2,1,128,256]{3,2,1,0:T(8,128)}, u32[]{:S(2)}) %copy-start) | copy-done | bytes 262168
  1.6 0.0 copy-start.1
  1.7 0.9 %copy-done.1 = f32[1,128,256]{2,1,0:T(8,128)S(1)} copy-done((f32[1,128,256]{2,1,0:T(8,128)S(1)}, f32[1,128,256]{2,1,0:T(8,128)}, u32[]{:S(2)}) %copy-start.1) | copy-done | bytes 131096
  2.6 0.0 copy-start.2
  2.6 0.9 %copy-done.2 = f32[1,128,256]{2,1,0:T(8,128)S(1)} copy-done((f32[1,128,256]{2,1,0:T(8,128)S(1)}, f32[1,128,256]{2,1,0:T(8,128)}, u32[]{:S(2)}) %copy-start.2) | copy-done | bytes 131096
  3.5 0.0 copy-start.3
  3.5 0.9 %copy-done.3 = s32[1,128,256]{2,1,0:T(8,128)S(1)} copy-done((s32[1,128,256]{2,1,0:T(8,128)S(1)}, s32[1,128,256]{2,1,0:T(8,128)}, u32[]{:S(2)}) %copy-start.3) | copy-done | bytes 131096
  4.4 0.0 copy-start.4
  4.4 0.9 %copy-done.4 = s32[1,128,256]{2,1,0:T(8,128)S(1)} copy-done((s32[1,128,256]{2,1,0:T(8,128)S(1)}, s32[1,128,256]{2,1,0:T(8,128)}, u32[]{:S(2)}) %copy-start.4) | copy-done | bytes 131096
  5.3 18.5 %shard_map.82 = f32[4,1,128,256]{3,2,1,0:T(8,128)S(1)} custom-call(f32[1,128,256]{2,1,0:T(8,128)S(1)} %copy-done.1, f32[2,1,128,256]{3,2,1,0:T(8,128)S(1)} %copy-done, f32[1,128,256]{2,1,0:T(8,128)S(1)} %copy-done.2, s32[1,128,256]{2,1,0:T(8,128)S(1)} %copy-done.3, s32[1,128,256]{2,1,0:T(8,128)S(1)} %copy-done.4, s32[2,128]{1,0:T(2,128)S(1)} %bitcast.2, ...), custom_call_target="tpu_custom_call" | custom-call | tf_op jit(solution)/shard_map/pallas_call | solution.py:425
  23.8 0.8 %copy.10 = f32[4,1,128,256]{3,2,1,0:T(8,128)} copy(f32[4,1,128,256]{3,2,1,0:T(8,128)S(1)} %shard_map.82) | data formatting | bytes 1048576
Async XLA Ops:
  0.0 0.7 %copy-start.6 = (s32[256]{0:T(256)S(1)}, s32[256]{0:T(256)}, u32[]{:S(2)}) copy-start(s32[256]{0:T(256)} %param.14) | copy-start | bytes 3076
  0.0 0.7 %copy-start.5 = (s32[256]{0:T(256)S(1)}, s32[256]{0:T(256)}, u32[]{:S(2)}) copy-start(s32[256]{0:T(256)} %param.13) | copy-start | bytes 3076
  0.0 0.7 %copy-start.7 = (f32[1,128]{1,0:T(1,128)S(1)}, f32[1,128]{1,0:T(1,128)}, u32[]{:S(2)}) copy-start(f32[1,128]{1,0:T(1,128)} %shift_ref.1) | copy-start | bytes 1540
  0.7 1.0 %copy-start = (f32[2,1,128,256]{3,2,1,0:T(8,128)S(1)}, f32[2,1,128,256]{3,2,1,0:T(8,128)}, u32[]{:S(2)}) copy-start(f32[2,1,128,256]{3,2,1,0:T(8,128)} %velocity_in.1) | copy-start | bytes 786436
  1.6 0.9 %copy-start.1 = (f32[1,128,256]{2,1,0:T(8,128)S(1)}, f32[1,128,256]{2,1,0:T(8,128)}, u32[]{:S(2)}) copy-start(f32[1,128,256]{2,1,0:T(8,128)} %density_in.1) | copy-start | bytes 393220
  2.6 0.9 %copy-start.2 = (f32[1,128,256]{2,1,0:T(8,128)S(1)}, f32[1,128,256]{2,1,0:T(8,128)}, u32[]{:S(2)}) copy-start(f32[1,128,256]{2,1,0:T(8,128)} %energy_in.1) | copy-start | bytes 393220
  3.5 0.9 %copy-start.3 = (s32[1,128,256]{2,1,0:T(8,128)S(1)}, s32[1,128,256]{2,1,0:T(8,128)}, u32[]{:S(2)}) copy-start(s32[1,128,256]{2,1,0:T(8,128)} %material_in.1) | copy-start | bytes 393220
  4.4 0.9 %copy-start.4 = (s32[1,128,256]{2,1,0:T(8,128)S(1)}, s32[1,128,256]{2,1,0:T(8,128)}, u32[]{:S(2)}) copy-start(s32[1,128,256]{2,1,0:T(8,128)} %limiter_in.1) | copy-start | bytes 393220

commit v2 on v1

--- a/solution.py
+++ b/solution.py
@@ -88,11 +88,11 @@
 
 def kernel(
     n_gx, n_gy,
-    density_in, velocity_in, energy_in, material_in, limiter_in, owners_ref, dest_ref, shift_ref, out_ref,
-    rho, spx, spy, ene, mat, lim, zed, pre, pl_x, pr_x, pl_y, pu_y, node_x, node_y, shift_b, turn_b,
-    to_left, to_right, from_left, from_right, base, outer_up, outer_down, from_down, from_up,
+    density_in, velocity_in, energy_in, material_in, limiter_in, owners_in, dest_in, shift_in, out_ref,
+    owners_ref, dest_ref, shift_ref, rho, spx, spy, ene, mat, lim, zed, pre, pl_x, pr_x, pl_y, pu_y, node_x, node_y, shift_b, turn_b,
+    to_left, to_right, from_left, from_right, outer_up, outer_down, from_down, from_up,
     seam_out_l, seam_out_r, seam_in_l, seam_in_r, rim,
-    in_sem, out_sem, bulk_send, bulk_recv, row_send, row_recv, seam_send, seam_recv,
+    in_sem, bulk_send, bulk_recv, row_send, row_recv, seam_send, seam_recv,
 ):
     gx = lax.axis_index("gx")
     gy = lax.axis_index("gy")
@@ -111,6 +111,9 @@
                 (velocity_in.at[0, 0], spx),
                 (velocity_in.at[1, 0], spy),
                 (limiter_in.at[0], lim),
+                (owners_in, owners_ref),
+                (dest_in, dest_ref),
+                (shift_in, shift_ref),
             )
         )
     ]
@@ -123,18 +126,6 @@
 
     lanes = lax.broadcasted_iota(jnp.int32, (ROWS, TILE), 1)
     rows = lax.broadcasted_iota(jnp.int32, (ROWS, TILE), 0)
-
-    turn_pairs = jnp.where(owners_ref[...] == gx, lax.bitwise_and(dest_ref[...], 1), -1).astype(jnp.float32)
-    turn_row = jnp.zeros((8, ROWS), jnp.float32)
-    for j in range(2):
-        pick = jnp.where(TILE * j + rows == 2 * lanes, 1.0, 0.0)
-        turn_row += jnp.dot(
-            jnp.broadcast_to(turn_pairs[j : j + 1], (8, TILE)), pick, preferred_element_type=jnp.float32
-        )
-    turn_row = turn_row[0:1]
-    turn_b[...] = jnp.transpose(jnp.broadcast_to(turn_row, (ROWS, ROWS)))
-    shift_row = shift_ref[...]
-    shift_b[...] = jnp.transpose(jnp.broadcast_to(shift_row, (ROWS, ROWS)))
 
     def wide(ref, start):
         return jnp.concatenate([ref[0, pl.ds(start, G), :], ref[1, pl.ds(start, G), :]], axis=1)
@@ -194,7 +185,7 @@
         return carry
 
     def over(first, last, step):
-        lax.fori_loop(first, last, step, None)
+        lax.fori_loop(first, last, step, None, unroll=min(4, last - first))
 
     sends = []
 
@@ -216,6 +207,19 @@
 
     for load in loads:
         load.wait()
+
+    turn_pairs = jnp.where(owners_ref[...] == gx, lax.bitwise_and(dest_ref[...], 1), -1).astype(jnp.float32)
+    turn_row = jnp.zeros((8, ROWS), jnp.float32)
+    for j in range(2):
+        pick = jnp.where(TILE * j + rows == 2 * lanes, 1.0, 0.0)
+        turn_row += jnp.dot(
+            jnp.broadcast_to(turn_pairs[j : j + 1], (8, TILE)), pick, preferred_element_type=jnp.float32
+        )
+    turn_row = turn_row[0:1]
+    turn_b[...] = jnp.transpose(jnp.broadcast_to(turn_row, (ROWS, ROWS)))
+    shift_row = shift_ref[...]
+    shift_b[...] = jnp.transpose(jnp.broadcast_to(shift_row, (ROWS, ROWS)))
+
 
     filler = jnp.ones((G, TILE), jnp.float32)
     for ref in (zed, pl_x, pr_x, pl_y, pu_y):
@@ -385,30 +389,23 @@
                 else:
                     value = jnp.where(turn == 0.0, second, jnp.where(turn == 1.0, first, 0.0))
                 extra = pltpu.roll(edge, (2 * TILE - 8 * q - 4) % TILE, 1)
-                base[f, here, half * TILE : (half + 1) * TILE] = value + jnp.where(near_edge, extra, 0.0)
+                out_ref[f, 0, here, half * TILE : (half + 1) * TILE] = value + jnp.where(near_edge, extra, 0.0)
         return carry
 
     def finish(g, carry=None):
         here = pl.ds(pl.multiple_of(g * G, G), G)
         turn = turn_b[here, :]
         for f in range(4):
-            base[f, here, :TILE] += jnp.where(turn == 1.0, from_left[f, here, :], 0.0)
-            base[f, here, TILE:] += jnp.where(turn == -1.0, from_right[f, here, :], 0.0)
+            out_ref[f, 0, here, :TILE] += jnp.where(turn == 1.0, from_left[f, here, :], 0.0)
+            out_ref[f, 0, here, TILE:] += jnp.where(turn == -1.0, from_right[f, here, :], 0.0)
         return carry
 
     over(0, 16, prepare)
 
-    outs = []
     for i, (first, last) in enumerate(((1, 5), (5, 9), (9, 13), (13, 15), (0, 1), (15, 16))):
         sends[2 * i].wait()
         sends[2 * i + 1].wait()
         over(first, last, finish)
-        there = pl.ds(first * G, (last - first) * G)
-        out = pltpu.make_async_copy(base.at[:, there, :], out_ref.at[:, 0, there, :], out_sem.at[i])
-        out.start()
-        outs.append(out)
-    for out in outs:
-        out.wait()
 
 
 def on_device(n_gx, n_gy, density, velocity, energy, material, limiter, owners, dest_tile, tile_shift):
@@ -420,23 +417,24 @@
     square = pltpu.VMEM((ROWS, TILE), f32)
     small = pltpu.VMEM((8, TILE), f32)
     seam = pltpu.VMEM((32, ROWS), f32)
-    any_space = pl.BlockSpec(memory_space=pl.ANY)
+    any_space = pl.BlockSpec(memory_space=pltpu.HBM)
     vmem = pl.BlockSpec(memory_space=pltpu.VMEM)
     return pl.pallas_call(
         functools.partial(kernel, n_gx, n_gy),
-        out_shape=jax.ShapeDtypeStruct((4, 1, ROWS, COLS), f32),
-        in_specs=[any_space] * 5 + [vmem] * 3,
-        out_specs=any_space,
+        out_shape=pltpu.VMEM((4, 1, ROWS, COLS), f32),
+        in_specs=[any_space] * 8,
+        out_specs=vmem,
         scratch_shapes=[
+            pltpu.VMEM((2, TILE), jnp.int32), pltpu.VMEM((2, TILE), jnp.int32), pltpu.VMEM((1, ROWS), f32),
             block, block, block, block,
             pltpu.VMEM((ROWS, COLS), jnp.int32), pltpu.VMEM((ROWS, COLS), jnp.int32),
             padded, block, padded, padded, padded, padded, padded, padded, square, square,
-            tiles, tiles, tiles, tiles, pltpu.VMEM((4, ROWS, COLS), f32),
+            tiles, tiles, tiles, tiles,
             small, small, small, small, seam, seam, seam, seam, square,
-            dma((6,)), dma((6,)), dma((2, 6)), dma((2, 6)), dma((2,)), dma((2,)), dma((2,)), dma((2,)),
+            dma((9,)), dma((2, 6)), dma((2, 6)), dma((2,)), dma((2,)), dma((2,)), dma((2,)),
         ],
         compiler_params=pltpu.CompilerParams(
-            collective_id=0, has_side_effects=True, vmem_limit_bytes=24 * 1024 * 1024
+            collective_id=0, has_side_effects=True, vmem_limit_bytes=58 * 1024 * 1024
         ),
     )(
         density, velocity, energy, material, limiter,

time: 24.8 us -> 16.8 us (0.68)
  local copies, waits for them, and re-layouts: 6.06 us -> 0.8 us
  Pallas kernels: 18.5 us -> 15.7 us
    unnamed x17 -> x1, local copies, waits for them, and re-layouts: 6.06 us -> 0.8 us
    pallas_call x1, Pallas kernels: 18.5 us -> 15.7 us  [on_device(): pl.pallas_call(functools.partial(kernel, n_gx, n_gy), out_shape=pltpu.VME...]
where the time goes in v2:
time: 16.8 us; the launch traced here: 16.5 us
  Pallas kernels  15.7 us (93%)
  local copies, waits for them, and re-layouts  0.8 us (5%)
    pallas_call x1, Pallas kernels, on_device(): pl.pallas_call(functools.partial(kernel, n_gx, n_gy), out_shape=pltpu.VME...  15.7 us
    unnamed x1, local copies, waits for them, and re-layouts  0.8 us

profile of v2, /device:TPU:0, one launch (start us, length us, event | category | flops | bytes accessed | tf_op | source)
XLA Modules:
  0.0 16.5 jit_solution(12291983971721787529)
XLA Ops:
  0.0 15.7 %shard_map.82 = f32[4,1,128,256]{3,2,1,0:T(8,128)S(1)} custom-call(f32[1,128,256]{2,1,0:T(8,128)} %density_in.1, f32[2,1,128,256]{3,2,1,0:T(8,128)} %velocity_in.1, f32[1,128,256]{2,1,0:T(8,128)} %energy_in.1, s32[1,128,256]{2,1,0:T(8,128)} %material_in.1, s32[1,128,256]{2,1,0:T(8,128)} %limiter_in.1, s32[2,128]{1,0:T(2,128)} %bitcast.2, s32[2,128]{1,0:T(2,128)} %bitcast.3, ...), custom_call_target="tpu_custom_call" | custom-call | tf_op jit(solution)/shard_map/pallas_call | solution.py:422
  15.7 0.8 %copy.10 = f32[4,1,128,256]{3,2,1,0:T(8,128)} copy(f32[4,1,128,256]{3,2,1,0:T(8,128)S(1)} %shard_map.82) | data formatting | bytes 1048576

commit v3 on v1

--- a/solution.py
+++ b/solution.py
@@ -16,6 +16,9 @@
 time_step = 0.05
 
 RUNS = ((1, 5), (5, 9), (9, 13), (13, 15))
+EARLY = 6
+DETOURS = {1: 2, 5: 2, 9: 2}
+RELAY = 3
 
 
 def by_material(material, first, second, third):
@@ -88,11 +91,11 @@
 
 def kernel(
     n_gx, n_gy,
-    density_in, velocity_in, energy_in, material_in, limiter_in, owners_ref, dest_ref, shift_ref, out_ref,
-    rho, spx, spy, ene, mat, lim, zed, pre, pl_x, pr_x, pl_y, pu_y, node_x, node_y, shift_b, turn_b,
-    to_left, to_right, from_left, from_right, base, outer_up, outer_down, from_down, from_up,
-    seam_out_l, seam_out_r, seam_in_l, seam_in_r, rim,
-    in_sem, out_sem, bulk_send, bulk_recv, row_send, row_recv, seam_send, seam_recv,
+    density_in, velocity_in, energy_in, material_in, limiter_in, owners_in, dest_in, shift_in, out_ref,
+    owners_ref, dest_ref, shift_ref, rho, spx, spy, ene, mat, lim, zed, pre, pl_x, pr_x, pl_y, pu_y, node_x, node_y, shift_b, turn_b,
+    to_left, to_right, from_left, from_right, outer, from_down, from_up, corner_ld, corner_lu, corner_rd, corner_ru,
+    seam_out_l, seam_out_r, seam_in_l, seam_in_r, rim, passing,
+    in_sem, bulk_send, bulk_recv, row_send, row_recv, corner_send, corner_recv, seam_send, seam_recv, relay_send, relay_recv,
 ):
     gx = lax.axis_index("gx")
     gy = lax.axis_index("gy")
@@ -101,40 +104,50 @@
     up_y = lax.rem(gy + 1, n_gy)
     down_y = lax.rem(gy + n_gy - 1, n_gy)
 
+    small_loads = [
+        pltpu.make_async_copy(source, target, in_sem.at[0, 6 + k])
+        for k, (source, target) in enumerate(((shift_in, shift_ref), (owners_in, owners_ref), (dest_in, dest_ref)))
+    ]
+    fields = (
+        (density_in.at[0], rho),
+        (energy_in.at[0], ene),
+        (material_in.at[0], mat),
+        (velocity_in.at[0, 0], spx),
+        (velocity_in.at[1, 0], spy),
+        (limiter_in.at[0], lim),
+    )
+    slabs = (pl.ds(0, EARLY * G), pl.ds(ROWS - G, G), pl.ds(EARLY * G, ROWS - G - EARLY * G))
     loads = [
-        pltpu.make_async_copy(source, target, in_sem.at[i])
-        for i, (source, target) in enumerate(
-            (
-                (density_in.at[0], rho),
-                (energy_in.at[0], ene),
-                (material_in.at[0], mat),
-                (velocity_in.at[0, 0], spx),
-                (velocity_in.at[1, 0], spy),
-                (limiter_in.at[0], lim),
-            )
-        )
+        [pltpu.make_async_copy(source.at[part, :], target.at[part, :], in_sem.at[i, k]) for k, (source, target) in enumerate(fields)]
+        for i, part in enumerate(slabs)
     ]
-    for load in loads:
+    for load in small_loads[:1] + loads[0] + loads[1] + loads[2] + small_loads[1:]:
         load.start()
 
+    has_up = gy < n_gy - 1
+    has_down = gy > 0
     barrier = pltpu.get_barrier_semaphore()
-    for target in ((left_x, gy), (right_x, gy), (gx, up_y), (gx, down_y)):
-        pl.semaphore_signal(barrier, inc=1, device_id=target, device_id_type=MESH)
+
+    def greet(column, level):
+        pl.semaphore_signal(barrier, inc=1, device_id=(column, level), device_id_type=MESH)
+
+    greet(left_x, gy)
+    greet(right_x, gy)
+    pl.when(has_up)(lambda: greet(gx, up_y))
+    pl.when(has_down)(lambda: greet(gx, down_y))
+    is_last = gx == n_gx - 1
+    is_relay = gx == RELAY
+    pl.when(is_relay)(lambda: greet(n_gx - 1, gy))
+
+    @pl.when(gx == 0)
+    def _():
+        greet(RELAY, gy)
+        pl.when(has_up)(lambda: greet(left_x, up_y))
+        pl.when(has_down)(lambda: greet(left_x, down_y))
+
 
     lanes = lax.broadcasted_iota(jnp.int32, (ROWS, TILE), 1)
     rows = lax.broadcasted_iota(jnp.int32, (ROWS, TILE), 0)
-
-    turn_pairs = jnp.where(owners_ref[...] == gx, lax.bitwise_and(dest_ref[...], 1), -1).astype(jnp.float32)
-    turn_row = jnp.zeros((8, ROWS), jnp.float32)
-    for j in range(2):
-        pick = jnp.where(TILE * j + rows == 2 * lanes, 1.0, 0.0)
-        turn_row += jnp.dot(
-            jnp.broadcast_to(turn_pairs[j : j + 1], (8, TILE)), pick, preferred_element_type=jnp.float32
-        )
-    turn_row = turn_row[0:1]
-    turn_b[...] = jnp.transpose(jnp.broadcast_to(turn_row, (ROWS, ROWS)))
-    shift_row = shift_ref[...]
-    shift_b[...] = jnp.transpose(jnp.broadcast_to(shift_row, (ROWS, ROWS)))
 
     def wide(ref, start):
         return jnp.concatenate([ref[0, pl.ds(start, G), :], ref[1, pl.ds(start, G), :]], axis=1)
@@ -194,28 +207,46 @@
         return carry
 
     def over(first, last, step):
-        lax.fori_loop(first, last, step, None)
-
+        lax.fori_loop(first, last, step, None, unroll=min(4, last - first))
+
+    def remote(source, target, send_sem, recv_sem, column, level=gy):
+        return pltpu.make_async_remote_copy(
+            src_ref=source, dst_ref=target, send_sem=send_sem, recv_sem=recv_sem,
+            device_id=(column, level), device_id_type=MESH,
+        )
+
+    parts = []
     sends = []
-
-    def send_rows(i, first, count):
-        there = pl.ds(first * G, count * G)
-        for way, (source, target, device) in enumerate(
-            ((to_right, from_left, right_x), (to_left, from_right, left_x))
-        ):
-            copy = pltpu.make_async_remote_copy(
-                src_ref=source.at[:, there, :],
-                dst_ref=target.at[:, there, :],
-                send_sem=bulk_send.at[way, i],
-                recv_sem=bulk_recv.at[way, i],
-                device_id=(device, gy),
-                device_id_type=MESH,
-            )
-            copy.start()
-            sends.append(copy)
-
-    for load in loads:
-        load.wait()
+    around, onward = [], []
+
+    def send_part(first, last, detour=False):
+        i = len(parts)
+        parts.append((first, last))
+        there = pl.ds(first * G, (last - first) * G)
+        go_right = remote(
+            to_right.at[:, there, :], from_left.at[:, there, :], bulk_send.at[0, i], bulk_recv.at[0, i], right_x
+        )
+        go_left = remote(
+            to_left.at[:, there, :], from_right.at[:, there, :], bulk_send.at[1, i], bulk_recv.at[1, i], left_x
+        )
+        sends.extend((go_right, go_left))
+        if detour:
+            k = len(around)
+            stop = passing.at[k, :, pl.ds(0, (last - first) * G), :]
+            around.append(remote(to_right.at[:, there, :], stop, bulk_send.at[0, i], relay_recv.at[k], RELAY))
+            onward.append(remote(stop, from_left.at[:, there, :], relay_send.at[k], bulk_recv.at[0, i], 0))
+            pl.when(is_last)(lambda: around[k].start())
+            pl.when(jnp.logical_not(is_last))(lambda: go_right.start())
+        else:
+            go_right.start()
+        go_left.start()
+
+    def send_run(first, last):
+        extra = DETOURS.get(first, 0)
+        if extra:
+            send_part(first, first + extra, True)
+        if first + extra < last:
+            send_part(first + extra, last)
 
     filler = jnp.ones((G, TILE), jnp.float32)
     for ref in (zed, pl_x, pr_x, pl_y, pu_y):
@@ -223,39 +254,66 @@
             ref[half, 0:G, :] = filler
             ref[half, ROWS + PAD : ROWS + PAD + G, :] = filler
 
+    small_loads[0].wait()
+    shift_row = shift_ref[...]
+    shift_b[...] = jnp.transpose(jnp.broadcast_to(shift_row, (ROWS, ROWS)))
+
+    for load in loads[0] + loads[1]:
+        load.wait()
     derive(15)
     over(0, 6, derive)
-    over(1, 6, nodes)
 
     for half in range(2):
         for k, ref in enumerate((zed, pl_x, pr_x, pl_y)):
-            outer_up[4 * half + k : 4 * half + k + 1, :] = ref[half, ROWS + PAD - 1 : ROWS + PAD, :]
+            outer[4 * half + k : 4 * half + k + 1, :] = ref[half, ROWS + PAD - 1 : ROWS + PAD, :]
         for k, ref in enumerate((zed, pl_x, pr_x, pu_y)):
-            outer_down[4 * half + k : 4 * half + k + 1, :] = ref[half, PAD : PAD + 1, :]
-
+            outer[8 + 4 * half + k : 8 + 4 * half + k + 1, :] = ref[half, PAD : PAD + 1, :]
+    outer_turned = jnp.transpose(
+        jnp.concatenate([outer[0:16, :], jnp.zeros((ROWS - 16, TILE), jnp.float32)], axis=0)
+    )
+    outer[16:24, :] = outer_turned[0:8, :]
+    outer[24:32, :] = outer_turned[120:128, :]
+
+    over(1, 6, nodes)
     over(1, 5, cells)
 
-    pl.semaphore_wait(barrier, 4)
-
-    row_copies = []
-    for way, (source, target, device) in enumerate(((outer_up, from_down, up_y), (outer_down, from_up, down_y))):
-        copy = pltpu.make_async_remote_copy(
-            src_ref=source, dst_ref=target, send_sem=row_send.at[way], recv_sem=row_recv.at[way],
-            device_id=(gx, device), device_id_type=MESH,
-        )
+
+    beside_count = has_up.astype(jnp.int32) + has_down.astype(jnp.int32)
+    met = 2 + beside_count + jnp.where(is_last | is_relay, 1, 0) + jnp.where(is_last, beside_count, 0)
+    pl.semaphore_wait(barrier, met)
+
+    row_copies = (
+        remote(outer, from_down, row_send.at[0], row_recv.at[0], gx, up_y),
+        remote(outer, from_up, row_send.at[1], row_recv.at[1], gx, down_y),
+    )
+    straight = (
+        remote(outer.at[24:32, :], corner_ld, corner_send.at[0], corner_recv.at[0], right_x, up_y),
+        remote(outer.at[24:32, :], corner_lu, corner_send.at[1], corner_recv.at[1], right_x, down_y),
+    )
+
+    def beside(copies, flags, act):
+        for copy, flag in zip(copies, flags, strict=True):
+
+            @pl.when(flag)
+            def _(copy=copy):
+                act(copy)
+
+    def begin(copy):
         copy.start()
-        row_copies.append(copy)
-
-    send_rows(0, 1, 4)
-    for i, (first, last) in enumerate(RUNS[1:3]):
-        top = min(last + 1, 15)
-        over(first + 1, top, derive)
-        over(first + 1, last + 1, nodes)
-        over(first, last, cells)
-        send_rows(1 + i, first, last - first)
-    over(14, 15, derive)
-    over(14, 16, nodes)
-    over(13, 15, cells)
+
+    def has_come(copy):
+        copy.wait_recv()
+
+    def has_gone(copy):
+        copy.wait_send()
+
+    beside(row_copies, (has_up, has_down), begin)
+    pl.when(is_last)(lambda: beside(straight, (has_up, has_down), begin))
+
+    send_part(1, 3, True)
+    send_part(3, 5)
+    for load in loads[2] + small_loads[1:]:
+        load.wait()
 
     packed_l = jnp.zeros((ROWS, TILE), jnp.float32)
     packed_r = jnp.zeros((ROWS, TILE), jnp.float32)
@@ -265,44 +323,83 @@
         inside = (lanes >= 4 * f) & (lanes < 4 * f + 4)
         packed_l = jnp.where(inside, pltpu.roll(first, 4 * f, 1) if f else first, packed_l)
         packed_r = jnp.where(inside, pltpu.roll(last, 4 * f + 4, 1), packed_r)
-    seam_out_l[0:24, :] = jnp.transpose(packed_l)[0:24, :]
-    seam_out_r[0:24, :] = jnp.transpose(packed_r)[0:24, :]
-
-    for copy in row_copies:
-        copy.wait()
-    below = jnp.where(gy == 0, 0.0, from_down[...])
-    above = jnp.where(gy == n_gy - 1, 0.0, from_up[...])
+    seam_out_l[...] = jnp.transpose(packed_l)[0:24, :]
+    seam_out_r[...] = jnp.transpose(packed_r)[0:24, :]
+
+    seam_copies = (
+        remote(seam_out_r, seam_in_l, seam_send.at[0], seam_recv.at[0], right_x),
+        remote(seam_out_l, seam_in_r, seam_send.at[1], seam_recv.at[1], left_x),
+    )
+    for copy in seam_copies:
+        copy.start()
+
+    for i, (first, last) in enumerate(RUNS[1:3]):
+        top = min(last + 1, 15)
+        over(first + 1, top, derive)
+        over(first + 1, last + 1, nodes)
+        over(first, last, cells)
+        send_run(first, last)
+    over(14, 15, derive)
+    over(14, 16, nodes)
+    over(13, 15, cells)
+    send_run(13, 15)
+
+    @pl.when(jnp.logical_not(has_down))
+    def _():
+        from_down[...] = jnp.zeros_like(from_down)
+        corner_ld[...] = jnp.zeros_like(corner_ld)
+        corner_rd[...] = jnp.zeros_like(corner_rd)
+
+    @pl.when(jnp.logical_not(has_up))
+    def _():
+        from_up[...] = jnp.zeros_like(from_up)
+        corner_lu[...] = jnp.zeros_like(corner_lu)
+        corner_ru[...] = jnp.zeros_like(corner_ru)
+
+    beside(row_copies, (has_down, has_up), has_come)
+    onward_right = (
+        remote(from_down.at[24:32, :], corner_ld, corner_send.at[0], corner_recv.at[0], right_x),
+        remote(from_up.at[24:32, :], corner_lu, corner_send.at[1], corner_recv.at[1], right_x),
+    )
+    onward_left = (
+        remote(from_down.at[16:24, :], corner_rd, corner_send.at[2], corner_recv.at[2], left_x),
+        remote(from_up.at[16:24, :], corner_ru, corner_send.at[3], corner_recv.at[3], left_x),
+    )
+    pl.when(jnp.logical_not(is_last))(lambda: beside(onward_right, (has_down, has_up), begin))
+    beside(onward_left, (has_down, has_up), begin)
+    below = from_down[0:8, :]
+    above = from_up[8:16, :]
     for half in range(2):
         for k, ref in enumerate((zed, pl_x, pr_x, pl_y)):
             ref[half, PAD - 1 : PAD, :] = below[4 * half + k : 4 * half + k + 1, :]
         for k, ref in enumerate((zed, pl_x, pr_x, pu_y)):
             ref[half, ROWS + PAD : ROWS + PAD + 1, :] = above[4 * half + k : 4 * half + k + 1, :]
-    outer_turned = jnp.transpose(
-        jnp.concatenate([below, above, jnp.zeros((ROWS - 16, TILE), jnp.float32)], axis=0)
-    )
-    seam_out_l[24:32, :] = outer_turned[0:8, :]
-    seam_out_r[24:32, :] = outer_turned[120:128, :]
-
-    seam_copies = []
-    for way, (source, target, device) in enumerate(
-        ((seam_out_r, seam_in_l, right_x), (seam_out_l, seam_in_r, left_x))
-    ):
-        copy = pltpu.make_async_remote_copy(
-            src_ref=source, dst_ref=target, send_sem=seam_send.at[way], recv_sem=seam_recv.at[way],
-            device_id=(device, gy), device_id_type=MESH,
-        )
-        copy.start()
-        seam_copies.append(copy)
-    send_rows(3, 13, 2)
     nodes(0)
     nodes(16)
     cells(0)
     cells(15)
-    send_rows(4, 0, 1)
-    send_rows(5, 15, 1)
-
+    send_run(0, 1)
+    send_run(15, 16)
+
+    @pl.when(is_relay)
+    def _():
+        for arrival, departure in zip(around, onward, strict=True):
+            arrival.wait_recv()
+            departure.start()
+
+
+    turn_pairs = jnp.where(owners_ref[...] == gx, lax.bitwise_and(dest_ref[...], 1), -1).astype(jnp.float32)
+    turn_row = jnp.zeros((8, ROWS), jnp.float32)
+    for j in range(2):
+        pick = jnp.where(TILE * j + rows == 2 * lanes, 1.0, 0.0)
+        turn_row += jnp.dot(
+            jnp.broadcast_to(turn_pairs[j : j + 1], (8, TILE)), pick, preferred_element_type=jnp.float32
+        )
+    turn_row = turn_row[0:1]
+    turn_b[...] = jnp.transpose(jnp.broadcast_to(turn_row, (ROWS, ROWS)))
     for copy in seam_copies:
-        copy.wait()
+        copy.wait_recv()
+    beside(onward_right + onward_left, (has_down, has_up) * 2, has_come)
 
     sub8 = lax.broadcasted_iota(jnp.int32, (8, TILE), 0)
     lane8 = lax.broadcasted_iota(jnp.int32, (8, TILE), 1)
@@ -319,12 +416,11 @@
             slots.append(jnp.where(sub8 < 4, head, tail))
         return jnp.concatenate(slots, axis=0)
 
-    def seam_outer(column):
-        slots = []
-        for before, after, b_off in ((seam_in_l, seam_out_l, 4), (seam_out_r, seam_in_r, 4)):
-            head = turned(before[24:32, :], b_off)
-            tail = turned(after[24:32, :], 4)
-            slots.append(jnp.where(sub8 < 4, head, tail)[:, column : column + 1])
+    def seam_outer(before_l, after_l, before_r, after_r, lane):
+        slots = [
+            jnp.where(sub8 < 4, turned(before[...], 4)[:, lane + 4 : lane + 5], turned(after[...], 4)[:, lane : lane + 1])
+            for before, after in ((before_l, after_l), (before_r, after_r))
+        ]
         return jnp.concatenate(slots, axis=0)
 
     density, energy, speed_x, speed_y, material, limiter = [seam_field(f) for f in range(6)]
@@ -335,16 +431,14 @@
     at_first = first_lane == 0
     at_last = first_lane == ROWS - 1
 
-    is_before = lax.broadcasted_iota(jnp.int32, (16, 1), 0)
-    is_before = lax.rem(is_before, 8) < 4
-
-    def outer_value(k):
-        return jnp.where(is_before, seam_outer(4 + k), seam_outer(k))
-
+    lower = (corner_ld, from_down.at[16:24, :], from_down.at[24:32, :], corner_rd)
+    upper = (corner_lu, from_up.at[16:24, :], from_up.at[24:32, :], corner_ru)
     mine_l = (impedance, push_x + pressure, push_x - pressure, push_y + pressure)
     mine_u = (impedance, push_x + pressure, push_x - pressure, push_y - pressure)
-    under = [jnp.where(at_first, outer_value(k), pltpu.roll(x, 1, 1)) for k, x in enumerate(mine_l)]
-    over_it = [jnp.where(at_last, outer_value(8 + k), pltpu.roll(x, ROWS - 1, 1)) for k, x in enumerate(mine_u)]
+    under = [jnp.where(at_first, seam_outer(*lower, k), pltpu.roll(x, 1, 1)) for k, x in enumerate(mine_l)]
+    over_it = [
+        jnp.where(at_last, seam_outer(*upper, 8 + k), pltpu.roll(x, ROWS - 1, 1)) for k, x in enumerate(mine_u)
+    ]
 
     def seam_left(x):
         return pltpu.roll(x, 1, 0)
@@ -385,30 +479,35 @@
                 else:
                     value = jnp.where(turn == 0.0, second, jnp.where(turn == 1.0, first, 0.0))
                 extra = pltpu.roll(edge, (2 * TILE - 8 * q - 4) % TILE, 1)
-                base[f, here, half * TILE : (half + 1) * TILE] = value + jnp.where(near_edge, extra, 0.0)
+                out_ref[f, 0, here, half * TILE : (half + 1) * TILE] = value + jnp.where(near_edge, extra, 0.0)
         return carry
 
     def finish(g, carry=None):
         here = pl.ds(pl.multiple_of(g * G, G), G)
         turn = turn_b[here, :]
         for f in range(4):
-            base[f, here, :TILE] += jnp.where(turn == 1.0, from_left[f, here, :], 0.0)
-            base[f, here, TILE:] += jnp.where(turn == -1.0, from_right[f, here, :], 0.0)
+            out_ref[f, 0, here, :TILE] += jnp.where(turn == 1.0, from_left[f, here, :], 0.0)
+            out_ref[f, 0, here, TILE:] += jnp.where(turn == -1.0, from_right[f, here, :], 0.0)
         return carry
 
     over(0, 16, prepare)
 
-    outs = []
-    for i, (first, last) in enumerate(((1, 5), (5, 9), (9, 13), (13, 15), (0, 1), (15, 16))):
-        sends[2 * i].wait()
-        sends[2 * i + 1].wait()
+    for i, (first, last) in enumerate(parts):
+        sends[2 * i].wait_recv()
+        sends[2 * i + 1].wait_recv()
         over(first, last, finish)
-        there = pl.ds(first * G, (last - first) * G)
-        out = pltpu.make_async_copy(base.at[:, there, :], out_ref.at[:, 0, there, :], out_sem.at[i])
-        out.start()
-        outs.append(out)
-    for out in outs:
-        out.wait()
+
+    beside(row_copies, (has_up, has_down), has_gone)
+    beside(onward_left, (has_down, has_up), has_gone)
+    pl.when(is_last)(lambda: beside(straight, (has_up, has_down), has_gone))
+    pl.when(jnp.logical_not(is_last))(lambda: beside(onward_right, (has_down, has_up), has_gone))
+    for copy in (*seam_copies, *sends):
+        copy.wait_send()
+
+    @pl.when(is_relay)
+    def _():
+        for departure in onward:
+            departure.wait_send()
 
 
 def on_device(n_gx, n_gy, density, velocity, energy, material, limiter, owners, dest_tile, tile_shift):
@@ -419,24 +518,28 @@
     tiles = pltpu.VMEM((4, ROWS, TILE), f32)
     square = pltpu.VMEM((ROWS, TILE), f32)
     small = pltpu.VMEM((8, TILE), f32)
-    seam = pltpu.VMEM((32, ROWS), f32)
-    any_space = pl.BlockSpec(memory_space=pl.ANY)
+    seam = pltpu.VMEM((24, ROWS), f32)
+    outer = pltpu.VMEM((32, TILE), f32)
+    any_space = pl.BlockSpec(memory_space=pltpu.HBM)
     vmem = pl.BlockSpec(memory_space=pltpu.VMEM)
     return pl.pallas_call(
         functools.partial(kernel, n_gx, n_gy),
-        out_shape=jax.ShapeDtypeStruct((4, 1, ROWS, COLS), f32),
-        in_specs=[any_space] * 5 + [vmem] * 3,
-        out_specs=any_space,
+        out_shape=pltpu.VMEM((4, 1, ROWS, COLS), f32),
+        in_specs=[any_space] * 8,
+        out_specs=vmem,
         scratch_shapes=[
+            pltpu.VMEM((2, TILE), jnp.int32), pltpu.VMEM((2, TILE), jnp.int32), pltpu.VMEM((1, ROWS), f32),
             block, block, block, block,
             pltpu.VMEM((ROWS, COLS), jnp.int32), pltpu.VMEM((ROWS, COLS), jnp.int32),
             padded, block, padded, padded, padded, padded, padded, padded, square, square,
-            tiles, tiles, tiles, tiles, pltpu.VMEM((4, ROWS, COLS), f32),
-            small, small, small, small, seam, seam, seam, seam, square,
-            dma((6,)), dma((6,)), dma((2, 6)), dma((2, 6)), dma((2,)), dma((2,)), dma((2,)), dma((2,)),
+            tiles, tiles, tiles, tiles,
+            outer, outer, outer, small, small, small, small, seam, seam, seam, seam, square, pltpu.VMEM((len(DETOURS), 4, 4 * G, TILE), f32),
+            dma((3, 9)), dma((2, 10)), dma((2, 10)),
+            dma((2,)), dma((2,)), dma((4,)), dma((4,)), dma((2,)), dma((2,)),
+            dma((len(DETOURS),)), dma((len(DETOURS),)),
         ],
         compiler_params=pltpu.CompilerParams(
-            collective_id=0, has_side_effects=True, vmem_limit_bytes=24 * 1024 * 1024
+            collective_id=0, has_side_effects=True, vmem_limit_bytes=58 * 1024 * 1024
         ),
     )(
         density, velocity, energy, material, limiter,

time: 24.8 us -> 15.7 us (0.63)
  local copies, waits for them, and re-layouts: 6.06 us -> 0.8 us
  Pallas kernels: 18.5 us -> 14.8 us
    unnamed x17 -> x1, local copies, waits for them, and re-layouts: 6.06 us -> 0.8 us
    pallas_call x1, Pallas kernels: 18.5 us -> 14.8 us  [on_device(): pl.pallas_call(functools.partial(kernel, n_gx, n_gy), out_shape=pltpu.VME...]
where the time goes in v3:
time: 15.7 us; the launch traced here: 15.6 us
  Pallas kernels  14.8 us (94%)
  local copies, waits for them, and re-layouts  0.8 us (5%)
    pallas_call x1, Pallas kernels, on_device(): pl.pallas_call(functools.partial(kernel, n_gx, n_gy), out_shape=pltpu.VME...  14.8 us
    unnamed x1, local copies, waits for them, and re-layouts  0.8 us

profile of v3, /device:TPU:0, one launch (start us, length us, event | category | flops | bytes accessed | tf_op | source)
XLA Modules:
  0.0 15.6 jit_solution(17335142185539046631)
XLA Ops:
  0.0 14.8 %shard_map.82 = f32[4,1,128,256]{3,2,1,0:T(8,128)S(1)} custom-call(f32[1,128,256]{2,1,0:T(8,128)} %density_in.1, f32[2,1,128,256]{3,2,1,0:T(8,128)} %velocity_in.1, f32[1,128,256]{2,1,0:T(8,128)} %energy_in.1, s32[1,128,256]{2,1,0:T(8,128)} %material_in.1, s32[1,128,256]{2,1,0:T(8,128)} %limiter_in.1, s32[2,128]{1,0:T(2,128)} %bitcast.2, s32[2,128]{1,0:T(2,128)} %bitcast.3, ...), custom_call_target="tpu_custom_call" | custom-call | tf_op jit(solution)/shard_map/pallas_call | solution.py:525
  14.8 0.8 %copy.10 = f32[4,1,128,256]{3,2,1,0:T(8,128)} copy(f32[4,1,128,256]{3,2,1,0:T(8,128)S(1)} %shard_map.82) | data formatting | bytes 1048576

commit v4 on v3

--- a/solution.py
+++ b/solution.py
@@ -202,8 +202,8 @@
             jnp.concatenate([shift, shift], axis=1), inner, left, right,
         )
         for f in range(4):
-            to_left[f, here, :] = sums[f][:, :TILE]
-            to_right[f, here, :] = sums[f][:, TILE:]
+            to_left[g, f] = sums[f][:, :TILE]
+            to_right[g, f] = sums[f][:, TILE:]
         return carry
 
     def over(first, last, step):
@@ -222,19 +222,19 @@
     def send_part(first, last, detour=False):
         i = len(parts)
         parts.append((first, last))
-        there = pl.ds(first * G, (last - first) * G)
+        there = pl.ds(first, last - first)
         go_right = remote(
-            to_right.at[:, there, :], from_left.at[:, there, :], bulk_send.at[0, i], bulk_recv.at[0, i], right_x
+            to_right.at[there], from_left.at[there], bulk_send.at[0, i], bulk_recv.at[0, i], right_x
         )
         go_left = remote(
-            to_left.at[:, there, :], from_right.at[:, there, :], bulk_send.at[1, i], bulk_recv.at[1, i], left_x
+            to_left.at[there], from_right.at[there], bulk_send.at[1, i], bulk_recv.at[1, i], left_x
         )
         sends.extend((go_right, go_left))
         if detour:
             k = len(around)
-            stop = passing.at[k, :, pl.ds(0, (last - first) * G), :]
-            around.append(remote(to_right.at[:, there, :], stop, bulk_send.at[0, i], relay_recv.at[k], RELAY))
-            onward.append(remote(stop, from_left.at[:, there, :], relay_send.at[k], bulk_recv.at[0, i], 0))
+            stop = passing.at[k, pl.ds(0, last - first)]
+            around.append(remote(to_right.at[there], stop, bulk_send.at[0, i], relay_recv.at[k], RELAY))
+            onward.append(remote(stop, from_left.at[there], relay_send.at[k], bulk_recv.at[0, i], 0))
             pl.when(is_last)(lambda: around[k].start())
             pl.when(jnp.logical_not(is_last))(lambda: go_right.start())
         else:
@@ -471,7 +471,7 @@
         turn = turn_b[here, :]
         edge = rim[here, :]
         for f in range(4):
-            first, second = to_left[f, here, :], to_right[f, here, :]
+            first, second = to_left[g, f], to_right[g, f]
             for half in range(2):
                 q = 2 * f + half
                 if half == 0:
@@ -486,8 +486,8 @@
         here = pl.ds(pl.multiple_of(g * G, G), G)
         turn = turn_b[here, :]
         for f in range(4):
-            out_ref[f, 0, here, :TILE] += jnp.where(turn == 1.0, from_left[f, here, :], 0.0)
-            out_ref[f, 0, here, TILE:] += jnp.where(turn == -1.0, from_right[f, here, :], 0.0)
+            out_ref[f, 0, here, :TILE] += jnp.where(turn == 1.0, from_left[g, f], 0.0)
+            out_ref[f, 0, here, TILE:] += jnp.where(turn == -1.0, from_right[g, f], 0.0)
         return carry
 
     over(0, 16, prepare)
@@ -515,7 +515,7 @@
     f32 = jnp.float32
     block = pltpu.VMEM((ROWS, COLS), f32)
     padded = pltpu.VMEM((2, ROWS + 2 * PAD, TILE), f32)
-    tiles = pltpu.VMEM((4, ROWS, TILE), f32)
+    tiles = pltpu.VMEM((ROWS // G, 4, G, TILE), f32)
     square = pltpu.VMEM((ROWS, TILE), f32)
     small = pltpu.VMEM((8, TILE), f32)
     seam = pltpu.VMEM((24, ROWS), f32)
@@ -533,7 +533,7 @@
             pltpu.VMEM((ROWS, COLS), jnp.int32), pltpu.VMEM((ROWS, COLS), jnp.int32),
             padded, block, padded, padded, padded, padded, padded, padded, square, square,
             tiles, tiles, tiles, tiles,
-            outer, outer, outer, small, small, small, small, seam, seam, seam, seam, square, pltpu.VMEM((len(DETOURS), 4, 4 * G, TILE), f32),
+            outer, outer, outer, small, small, small, small, seam, seam, seam, seam, square, pltpu.VMEM((len(DETOURS), 4, 4, G, TILE), f32),
             dma((3, 9)), dma((2, 10)), dma((2, 10)),
             dma((2,)), dma((2,)), dma((4,)), dma((4,)), dma((2,)), dma((2,)),
             dma((len(DETOURS),)), dma((len(DETOURS),)),

time: 15.7 us -> 15.7 us (level)
  no operation moved by 1% of the time
where the time goes in v4:
time: 15.7 us; the launch traced here: 15.5 us
  Pallas kernels  14.7 us (94%)
  local copies, waits for them, and re-layouts  0.8 us (5%)
    pallas_call x1, Pallas kernels, on_device(): pl.pallas_call(functools.partial(kernel, n_gx, n_gy), out_shape=pltpu.VME...  14.7 us
    unnamed x1, local copies, waits for them, and re-layouts  0.8 us

profile of v4, /device:TPU:0, one launch (start us, length us, event | category | flops | bytes accessed | tf_op | source)
XLA Modules:
  0.0 15.5 jit_solution(7915455887210766954)
XLA Ops:
  0.0 14.7 %shard_map.82 = f32[4,1,128,256]{3,2,1,0:T(8,128)S(1)} custom-call(f32[1,128,256]{2,1,0:T(8,128)} %density_in.1, f32[2,1,128,256]{3,2,1,0:T(8,128)} %velocity_in.1, f32[1,128,256]{2,1,0:T(8,128)} %energy_in.1, s32[1,128,256]{2,1,0:T(8,128)} %material_in.1, s32[1,128,256]{2,1,0:T(8,128)} %limiter_in.1, s32[2,128]{1,0:T(2,128)} %bitcast.2, s32[2,128]{1,0:T(2,128)} %bitcast.3, ...), custom_call_target="tpu_custom_call" | custom-call | tf_op jit(solution)/shard_map/pallas_call | solution.py:525
  14.7 0.8 %copy.10 = f32[4,1,128,256]{3,2,1,0:T(8,128)} copy(f32[4,1,128,256]{3,2,1,0:T(8,128)S(1)} %shard_map.82) | data formatting | bytes 1048576

commit v5 on v4

--- a/solution.py
+++ b/solution.py
@@ -307,11 +307,11 @@
     def has_gone(copy):
         copy.wait_send()
 
+    send_part(1, 3, True)
     beside(row_copies, (has_up, has_down), begin)
+    send_part(3, 5)
     pl.when(is_last)(lambda: beside(straight, (has_up, has_down), begin))
 
-    send_part(1, 3, True)
-    send_part(3, 5)
     for load in loads[2] + small_loads[1:]:
         load.wait()
 

time: 15.7 us -> 15.7 us (level)
  no operation moved by 1% of the time
where the time goes in v5:
time: 15.7 us; the launch traced here: 15.5 us
  Pallas kernels  14.7 us (94%)
  local copies, waits for them, and re-layouts  0.8 us (5%)
    pallas_call x1, Pallas kernels, on_device(): pl.pallas_call(functools.partial(kernel, n_gx, n_gy), out_shape=pltpu.VME...  14.7 us
    unnamed x1, local copies, waits for them, and re-layouts  0.8 us

profile of v5, /device:TPU:0, one launch (start us, length us, event | category | flops | bytes accessed | tf_op | source)
XLA Modules:
  0.0 15.5 jit_solution(15869991986392925098)
XLA Ops:
  0.0 14.7 %shard_map.82 = f32[4,1,128,256]{3,2,1,0:T(8,128)S(1)} custom-call(f32[1,128,256]{2,1,0:T(8,128)} %density_in.1, f32[2,1,128,256]{3,2,1,0:T(8,128)} %velocity_in.1, f32[1,128,256]{2,1,0:T(8,128)} %energy_in.1, s32[1,128,256]{2,1,0:T(8,128)} %material_in.1, s32[1,128,256]{2,1,0:T(8,128)} %limiter_in.1, s32[2,128]{1,0:T(2,128)} %bitcast.2, s32[2,128]{1,0:T(2,128)} %bitcast.3, ...), custom_call_target="tpu_custom_call" | custom-call | tf_op jit(solution)/shard_map/pallas_call | solution.py:525
  14.7 0.8 %copy.10 = f32[4,1,128,256]{3,2,1,0:T(8,128)} copy(f32[4,1,128,256]{3,2,1,0:T(8,128)S(1)} %shard_map.82) | data formatting | bytes 1048576

commit v6 on v3

--- a/solution.py
+++ b/solution.py
@@ -235,11 +235,11 @@
             stop = passing.at[k, :, pl.ds(0, (last - first) * G), :]
             around.append(remote(to_right.at[:, there, :], stop, bulk_send.at[0, i], relay_recv.at[k], RELAY))
             onward.append(remote(stop, from_left.at[:, there, :], relay_send.at[k], bulk_recv.at[0, i], 0))
-            pl.when(is_last)(lambda: around[k].start())
-            pl.when(jnp.logical_not(is_last))(lambda: go_right.start())
+            pl.when(is_last & has_down)(lambda: around[k].start())
+            pl.when(jnp.logical_not(is_last) & has_down)(lambda: go_right.start())
         else:
-            go_right.start()
-        go_left.start()
+            pl.when(has_down)(lambda: go_right.start())
+        pl.when(has_up)(lambda: go_left.start())
 
     def send_run(first, last):
         extra = DETOURS.get(first, 0)
@@ -343,6 +343,14 @@
     over(14, 16, nodes)
     over(13, 15, cells)
     send_run(13, 15)
+
+    @pl.when(jnp.logical_not(has_down))
+    def _():
+        from_left[...] = jnp.zeros_like(from_left)
+
+    @pl.when(jnp.logical_not(has_up))
+    def _():
+        from_right[...] = jnp.zeros_like(from_right)
 
     @pl.when(jnp.logical_not(has_down))
     def _():
@@ -381,7 +389,7 @@
     send_run(0, 1)
     send_run(15, 16)
 
-    @pl.when(is_relay)
+    @pl.when(is_relay & has_down)
     def _():
         for arrival, departure in zip(around, onward, strict=True):
             arrival.wait_recv()
@@ -493,18 +501,21 @@
     over(0, 16, prepare)
 
     for i, (first, last) in enumerate(parts):
-        sends[2 * i].wait_recv()
-        sends[2 * i + 1].wait_recv()
+        pl.when(has_down)(lambda: sends[2 * i].wait_recv())
+        pl.when(has_up)(lambda: sends[2 * i + 1].wait_recv())
         over(first, last, finish)
 
     beside(row_copies, (has_up, has_down), has_gone)
     beside(onward_left, (has_down, has_up), has_gone)
     pl.when(is_last)(lambda: beside(straight, (has_up, has_down), has_gone))
     pl.when(jnp.logical_not(is_last))(lambda: beside(onward_right, (has_down, has_up), has_gone))
-    for copy in (*seam_copies, *sends):
+    for copy in seam_copies:
         copy.wait_send()
-
-    @pl.when(is_relay)
+    for go_right, go_left in zip(sends[0::2], sends[1::2], strict=True):
+        pl.when(has_down)(lambda: go_right.wait_send())
+        pl.when(has_up)(lambda: go_left.wait_send())
+
+    @pl.when(is_relay & has_down)
     def _():
         for departure in onward:
             departure.wait_send()

time: 15.7 us -> 15.7 us (level)
  the two profiles are of different devices: /device:TPU:0 before, /device:TPU:10 now
where the time goes in v6:
time: 15.7 us; the launch traced here: 15.5 us
  Pallas kernels  14.7 us (94%)
  local copies, waits for them, and re-layouts  0.8 us (5%)
    pallas_call x1, Pallas kernels, on_device(): pl.pallas_call(functools.partial(kernel, n_gx, n_gy), out_shape=pltpu.VME...  14.7 us
    unnamed x1, local copies, waits for them, and re-layouts  0.8 us

profile of v6, /device:TPU:10, one launch (start us, length us, event | category | flops | bytes accessed | tf_op | source)
XLA Modules:
  0.0 15.5 jit_solution(8831342504780828332)
XLA Ops:
  0.0 14.7 %shard_map.82 = f32[4,1,128,256]{3,2,1,0:T(8,128)S(1)} custom-call(f32[1,128,256]{2,1,0:T(8,128)} %density_in.1, f32[2,1,128,256]{3,2,1,0:T(8,128)} %velocity_in.1, f32[1,128,256]{2,1,0:T(8,128)} %energy_in.1, s32[1,128,256]{2,1,0:T(8,128)} %material_in.1, s32[1,128,256]{2,1,0:T(8,128)} %limiter_in.1, s32[2,128]{1,0:T(2,128)} %bitcast.2, s32[2,128]{1,0:T(2,128)} %bitcast.3, ...), custom_call_target="tpu_custom_call" | custom-call | tf_op jit(solution)/shard_map/pallas_call | solution.py:536
  14.7 0.8 %copy.10 = f32[4,1,128,256]{3,2,1,0:T(8,128)} copy(f32[4,1,128,256]{3,2,1,0:T(8,128)S(1)} %shard_map.82) | data formatting | bytes 1048576
